TPU v7x, 32 devices: a whole 2x2x4 slice. The times are simulated.
32 devices in a mesh: seq: 8 (over z, x), fsdp: 4 (over y, core).
Axes of the slice: x: 2, y: 2, z: 4, core: 2. Of those that a mesh axis runs over, the one named last changes fastest.
Arguments:
- tokens: bfloat16 [4, 1024, 4608], P('fsdp', 'seq'), may hold values from -6 to 6
- norm_gain: float32 [4608], replicated, may hold values from 0.3 to 3
- router_weight: float32 [4608], replicated, may hold values from -0.09375 to 0.09375
- w_query: bfloat16 [4608, 1024], P('fsdp', 'seq'), may hold values from -0.09375 to 0.09375
- w_key: bfloat16 [4608, 1024], P('fsdp', 'seq'), may hold values from -0.09375 to 0.09375
- w_value: bfloat16 [4608, 1024], P('fsdp', 'seq'), may hold values from -0.09375 to 0.09375
- w_out: bfloat16 [1024, 4608], P('seq', 'fsdp'), may hold values from -0.1875 to 0.1875
- cotangent: bfloat16 [4, 1024, 4608], P('fsdp', 'seq'), may hold values from -6 to 6
- kept_index: int32 [4, 8, 24], P('fsdp', 'seq'), may hold values from -1 to 127, as said below
Outputs:
- mixed_rows: bfloat16 [4, 1024, 4608], P('fsdp', 'seq')
- grad_tokens: bfloat16 [4, 1024, 4608], P('fsdp', 'seq')
- grad_query: float32 [4608, 1024], P('fsdp', 'seq')
- grad_key: float32 [4608, 1024], P('fsdp', 'seq')
- grad_value: float32 [4608, 1024], P('fsdp', 'seq')
- grad_out: float32 [1024, 4608], P('seq', 'fsdp')
- grad_gain: float32 [4608], replicated
- grad_router: float32 [4608], replicated
Inputs may be any that keep to these rules, and one draw needn't show every extreme that they name: `kept_index`: each row of a document and index of seq lists distinct increasing local positions, followed by -1 in its empty slots. Every document keeps exactly 128 tokens in all, and in every document some index of seq fills all 24 slots.
All inputs are finite; a program needn't handle non-finite values.
Results may differ from a plain program's by a relative error of at most 0.012.
The roundings to bfloat16 on the way count: a program that leaves them out, or rounds other values in their place, can miss the bound.
Values may be sent and summed in bfloat16 or wider, within the bound.
A program may use at most 64 MiB of HBM per device.

v0:
```python
import jax
import jax.numpy as jnp
from jax import lax
from jax.sharding import PartitionSpec as P

SOFTCAP = 50.0
QUERY_SCALE = 1.0 / 12.0
FAR = 2**30
EPS = 1e-06


def contract_rows(left, right):
    return lax.dot_general(
        left, right, (((0,), (0,)), ((), ())), preferred_element_type=jnp.float32
    )


def contract_cols(left, right):
    return lax.dot_general(
        left, right, (((1,), (1,)), ((), ())), preferred_element_type=jnp.float32
    )


def body(tokens, norm_gain, router_weight, w_query, w_key, w_value, w_out, cotangent, kept_index):
    own_rows = tokens.shape[1]
    slot_list = kept_index[0, 0]
    is_kept = slot_list >= 0
    picked = jnp.where(is_kept, slot_list, 0)
    kept_rows = jnp.where(is_kept[:, None], tokens[0][picked], jnp.zeros((), jnp.bfloat16))
    kept_float = kept_rows.astype(jnp.float32)
    inv_root = lax.rsqrt(jnp.mean(kept_float * kept_float, axis=1) + EPS)
    unit = kept_float * inv_root[:, None]
    seq_index = lax.axis_index("seq")
    position = jnp.where(is_kept, slot_list + seq_index * own_rows, FAR)
    sending = (unit * norm_gain).astype(jnp.bfloat16)
    all_rows, all_position = (
        lax.all_gather(sending, "seq", axis=0, tiled=True),
        lax.all_gather(position, "seq", axis=0, tiled=True),
    )
    query_cols, key_cols, value_cols = (
        lax.all_gather(w_query, "fsdp", axis=0, tiled=True),
        lax.all_gather(w_key, "fsdp", axis=0, tiled=True),
        lax.all_gather(w_value, "fsdp", axis=0, tiled=True),
    )
    out_full = lax.all_gather(w_out, "fsdp", axis=1, tiled=True)
    queries = jnp.dot(all_rows, query_cols, preferred_element_type=jnp.float32).astype(jnp.bfloat16)
    keys_all = jnp.dot(all_rows, key_cols, preferred_element_type=jnp.float32).astype(jnp.bfloat16)
    values_all = jnp.dot(all_rows, value_cols, preferred_element_type=jnp.float32).astype(
        jnp.bfloat16
    )
    raw_scores = contract_cols(queries, keys_all) * QUERY_SCALE
    capped = SOFTCAP * jnp.tanh(raw_scores / SOFTCAP)
    allowed = (all_position[None, :] <= all_position[:, None]) & (all_position[None, :] < FAR)
    powers = jnp.where(allowed, jnp.exp(capped), 0.0)
    softmax_values = powers / jnp.sum(powers, axis=1, keepdims=True)
    rounded_weights = softmax_values.astype(jnp.bfloat16)
    attended = jnp.dot(rounded_weights, values_all, preferred_element_type=jnp.float32).astype(
        jnp.bfloat16
    )
    mixed_sum = lax.psum_scatter(
        jnp.dot(attended, out_full, preferred_element_type=jnp.float32).astype(jnp.bfloat16),
        "seq",
        scatter_dimension=0,
        tiled=True,
    ).astype(jnp.float32)
    logits = jnp.dot(kept_float, router_weight, precision=lax.Precision.HIGHEST)
    gate_value = jax.nn.sigmoid(logits)
    new_rows = (kept_float + gate_value[:, None] * mixed_sum).astype(jnp.bfloat16)
    target = jnp.where(is_kept, slot_list, own_rows)
    mixed_rows = tokens[0].at[target].set(new_rows, mode="drop")[None]
    cot_rows = jnp.where(
        is_kept[:, None], cotangent[0][picked], jnp.zeros((), jnp.bfloat16)
    ).astype(jnp.float32)
    d_gate = jnp.sum(cot_rows * mixed_sum, axis=1)
    d_logit = d_gate * gate_value * (1.0 - gate_value)
    d_mix = (gate_value[:, None] * cot_rows).astype(jnp.bfloat16)
    d_mix_all = lax.all_gather(d_mix, "seq", axis=0, tiled=True)
    out_grad = lax.psum_scatter(
        contract_rows(attended, d_mix_all).astype(jnp.bfloat16),
        "fsdp",
        scatter_dimension=1,
        tiled=True,
    ).astype(jnp.float32)
    d_attended = contract_cols(d_mix_all, out_full).astype(jnp.bfloat16)
    d_values = contract_rows(rounded_weights, d_attended).astype(jnp.bfloat16)
    d_probs = contract_cols(d_attended, values_all)
    d_soft = softmax_values * (d_probs - jnp.sum(softmax_values * d_probs, axis=1, keepdims=True))
    d_raw = (d_soft * (1.0 - capped / SOFTCAP * (capped / SOFTCAP)) * QUERY_SCALE).astype(
        jnp.bfloat16
    )
    d_queries = jnp.dot(d_raw, keys_all, preferred_element_type=jnp.float32).astype(jnp.bfloat16)
    d_keys = contract_rows(d_raw, queries).astype(jnp.bfloat16)
    d_stack = jnp.concatenate([d_queries, d_keys, d_values], axis=1)
    head_width = w_query.shape[1]
    shares = lax.psum_scatter(
        contract_rows(all_rows, d_stack).astype(jnp.bfloat16),
        "fsdp",
        scatter_dimension=0,
        tiled=True,
    ).astype(jnp.float32)
    grad_query = shares[:, :head_width]
    grad_key = shares[:, head_width : 2 * head_width]
    grad_value = shares[:, 2 * head_width : 3 * head_width]
    total = contract_cols(d_queries, query_cols)
    total = total + contract_cols(d_keys, key_cols)
    d_normed = lax.psum_scatter(
        (total + contract_cols(d_values, value_cols)).astype(jnp.bfloat16),
        "seq",
        scatter_dimension=0,
        tiled=True,
    ).astype(jnp.float32)
    gain_term = jnp.sum(d_normed * unit, axis=0)
    router_term = jnp.sum(d_logit[:, None] * kept_float, axis=0)
    grad_gain, grad_router = lax.psum((gain_term, router_term), ("seq", "fsdp"))
    scaled = d_normed * norm_gain
    d_kept = inv_root[:, None] * (scaled - unit * jnp.mean(scaled * unit, axis=1, keepdims=True))
    grad_new = (cot_rows + d_kept + d_logit[:, None] * router_weight).astype(jnp.bfloat16)
    grad_tokens = cotangent[0].at[target].set(grad_new, mode="drop")[None]
    return (
        mixed_rows,
        grad_tokens,
        grad_query,
        grad_key,
        grad_value,
        out_grad,
        grad_gain,
        grad_router,
    )


def solution(mesh):
    in_specs = (
        P("fsdp", "seq", None),
        P(),
        P(),
        P("fsdp", "seq"),
        P("fsdp", "seq"),
        P("fsdp", "seq"),
        P("seq", "fsdp"),
        P("fsdp", "seq", None),
        P("fsdp", "seq", None),
    )
    out_specs = (
        P("fsdp", "seq", None),
        P("fsdp", "seq", None),
        P("fsdp", "seq"),
        P("fsdp", "seq"),
        P("fsdp", "seq"),
        P("seq", "fsdp"),
        P(),
        P(),
    )
    return jax.shard_map(body, mesh=mesh, in_specs=in_specs, out_specs=out_specs, check_vma=False)
```

profile of v0, /device:TPU:0, one launch (start us, length us, event | category | flops | bytes accessed | tf_op | source)
XLA Modules:
  0.0 405.5 jit_solution(18415844087111275177)
XLA Ops:
  15.2 13.1 %all-reduce = s32[192]{0:T(256)S(1)} all-reduce(s32[192]{0:T(256)S(1)} %fusion.43), channel_id=1, replica_groups=mesh['seq'=8,'fsdp'=4] {'seq'}, use_global_device_ids=true, to_apply=%add | all-reduce | flops 192 | bytes 1536
  28.2 1.5 all-gather.11.cloned.1.call-done
  29.8 48.7 %all-gather.7.cloned.1.call-done = bf16[192,4608]{1,0:T(8,128)(2,1)} async-done(((bf16[24,4608]{1,0:T(8,128)(2,1)}), bf16[192,4608]{1,0:T(8,128)(2,1)}) %all-gather.7.cloned.1.call-update) | async-done | bytes 1769488 | tf_op jit(solution)/shard_map/all_gather | solution.py:37
  78.5 2.5 convolution_convert_fusion.9
  81.0 15.5 %all-gather.9.cloned.1.call-done = bf16[4608,128]{1,0:T(8,128)(2,1)} async-done(((bf16[1152,128]{1,0:T(8,128)(2,1)}), bf16[4608,128]{1,0:T(8,128)(2,1)}) %all-gather.9.cloned.1.call-update) | async-done | bytes 1179664 | tf_op jit(solution)/shard_map/all_gather | solution.py:41
  96.5 1.9 convolution_convert_fusion.10
  98.7 16.7 %all-gather.13.cloned.1.call-done = bf16[4608,128]{1,0:T(8,128)(2,1)} async-done(((bf16[1152,128]{1,0:T(8,128)(2,1)}), bf16[4608,128]{1,0:T(8,128)(2,1)}) %all-gather.13.cloned.1.call-update) | async-done | bytes 1179664 | tf_op jit(solution)/shard_map/all_gather | solution.py:43
  115.5 1.9 convolution_convert_fusion.8
  118.3 16.1 %all-gather.15.cloned.1.call-done = bf16[128,4608]{1,0:T(8,128)(2,1)} async-done(((bf16[128,1152]{1,0:T(8,128)(2,1)}), bf16[128,4608]{1,0:T(8,128)(2,1)}) %all-gather.15.cloned.1.call-update) | async-done | bytes 1179664 | tf_op jit(solution)/shard_map/all_gather | solution.py:45
  134.4 3.1 convolution_convert_fusion.1
  140.6 63.6 %reduce-scatter.7.cloned.1.call-done = bf16[24,4608]{1,0:T(8,128)(2,1)} async-done(((bf16[192,4608]{1,0:T(8,128)(2,1)}), bf16[24,4608]{1,0:T(8,128)(2,1)}) %reduce-scatter.7.cloned.1.call-update) | async-done | bytes 221200 | tf_op jit(solution)/shard_map/reduce_scatter | solution.py:60
  204.2 2.4 fusion.15
  206.7 45.3 %all-gather.17.cloned.1.call-done = bf16[192,4608]{1,0:T(8,128)(2,1)} async-done(((bf16[24,4608]{1,0:T(8,128)(2,1)}), bf16[192,4608]{1,0:T(8,128)(2,1)}) %all-gather.17.cloned.1.call-update) | async-done | bytes 1769488 | tf_op jit(solution)/shard_map/all_gather | solution.py:77
  252.0 3.0 convolution_convert_fusion.2
  255.0 2.4 copy.17
  257.5 2.5 convolution_convert_fusion.6
  264.2 1.9 fusion
  266.1 3.2 convolution_convert_fusion
  270.6 1.8 scatter_custom_fusion
  272.5 9.9 %reduce-scatter.13.cloned.1.call-done = bf16[1152,128]{1,0:T(8,128)(2,1)} async-done(((bf16[4608,128]{1,0:T(8,128)(2,1)}), bf16[1152,128]{1,0:T(8,128)(2,1)}) %reduce-scatter.13.cloned.1.call-update) | async-done | bytes 294928
  284.4 67.4 %reduce-scatter.9.cloned.1.call-done = bf16[24,4608]{1,0:T(8,128)(2,1)} async-done(((bf16[192,4608]{1,0:T(8,128)(2,1)}), bf16[24,4608]{1,0:T(8,128)(2,1)}) %reduce-scatter.9.cloned.1.call-update) | async-done | bytes 221200 | tf_op jit(solution)/shard_map/reduce_scatter | solution.py:106
  353.2 2.2 scatter_custom_fusion.1
  355.5 40.8 %all-reduce.1 = (f32[4608]{0:T(1024)}, f32[4608]{0:T(1024)}) all-reduce(f32[4608]{0:T(1024)S(1)} %get-tuple-element.8, f32[4608]{0:T(1024)S(1)} %get-tuple-element.10), channel_id=1, replica_groups=mesh['seq'=8,'fsdp'=4] {'seq','fsdp'}, use_global_device_ids=true, to_apply=%region_12.13 | all-reduce | flops 9216 | bytes 73728 | tf_op jit(solution)/shard_map/psum | solution.py:114
  396.3 2.4 fusion.47
  (101 shorter events, 20.4 us)
Async XLA Ops:
  7.2 22.6 %all-gather.11.cloned.1.call-start = ((), (), s32[]{:S(2)}) async-start(), calls=%async_computation.6 | async-start | bytes 1474560 | tf_op jit(solution)/shard_map/all_gather | solution.py:42
  9.0 69.5 %all-gather.7.cloned.1.call-start = ((), (), s32[]{:S(2)}) async-start(), calls=%async_computation.4 | async-start | bytes 1990656 | tf_op jit(solution)/shard_map/all_gather | solution.py:37
  10.7 3.1 copy-start.24
  11.8 84.7 %all-gather.9.cloned.1.call-start = ((), (), s32[]{:S(2)}) async-start(), calls=%async_computation.5 | async-start | bytes 1474560 | tf_op jit(solution)/shard_map/all_gather | solution.py:41
  12.6 102.9 %all-gather.13.cloned.1.call-start = ((), (), s32[]{:S(2)}) async-start(), calls=%async_computation.7 | async-start | bytes 1474560 | tf_op jit(solution)/shard_map/all_gather | solution.py:43
  13.2 121.2 %all-gather.15.cloned.1.call-start = ((), (), s32[]{:S(2)}) async-start(), calls=%async_computation.8 | async-start | bytes 1474560 | tf_op jit(solution)/shard_map/all_gather | solution.py:45
  13.7 190.5 %reduce-scatter.7.cloned.1.call-start = ((), (), s32[]{:S(2)}) async-start(), calls=%async_computation.9 | async-start | bytes 1990656 | tf_op jit(solution)/shard_map/reduce_scatter | solution.py:60
  28.2 89.1 %copy-start.20 = (pred[192]{0:T(512)(128)(4,1)}, pred[192]{0:T(512)(128)(4,1)S(1)}, u32[]{:S(2)}) copy-start(pred[192]{0:T(512)(128)(4,1)S(1)} %broadcast_compare_fusion) | copy-start | bytes 580
  78.5 18.1 %copy-start = (bf16[192,4608]{1,0:T(8,128)(2,1)S(1)}, bf16[192,4608]{1,0:T(8,128)(2,1)}, u32[]{:S(2)}) copy-start(bf16[192,4608]{1,0:T(8,128)(2,1)} %all-gather.7.cloned.1.call-done) | copy-start | bytes 5308420
  98.7 18.7 %copy-start.10 = (f32[192,192]{0,1:T(8,128)}, f32[192,192]{0,1:T(8,128)S(1)}, u32[]{:S(2)}) copy-start(f32[192,192]{0,1:T(8,128)S(1)} %get-tuple-element.21) | copy-start | bytes 442372
  98.7 18.7 %copy-start.18 = (f32[192]{0:T(256)}, f32[192]{0:T(256)S(1)}, u32[]{:S(2)}) copy-start(f32[192]{0:T(256)S(1)} %get-tuple-element.20) | copy-start | bytes 2308
  137.5 114.5 %all-gather.17.cloned.1.call-start = ((), (), s32[]{:S(2)}) async-start(), calls=%async_computation.10 | async-start | bytes 1990656 | tf_op jit(solution)/shard_map/all_gather | solution.py:77
  206.7 75.8 %reduce-scatter.13.cloned.1.call-start = ((), (), s32[]{:S(2)}) async-start(), calls=%async_computation.13 | async-start | bytes 1474560
  257.4 2.6 copy-start.17
  257.4 94.4 %reduce-scatter.9.cloned.1.call-start = ((), (), s32[]{:S(2)}) async-start(), calls=%async_computation.11 | async-start | bytes 1990656 | tf_op jit(solution)/shard_map/reduce_scatter | solution.py:106
  257.5 2.5 copy-start.11
  257.5 2.5 copy-start.19
  257.5 2.5 copy-start.21
  266.1 130.2 %reduce-scatter.11.cloned.1.call-start = ((), (), s32[]{:S(2)}) async-start(), calls=%async_computation.12 | async-start | bytes 4423680 | tf_op jit(solution)/shard_map/reduce_scatter | solution.py:95
  269.3 3.1 copy-start.22
  270.6 81.2 %copy-start.13 = (f32[4608]{0:T(1024)S(1)}, f32[4608]{0:T(1024)}, u32[]{:S(2)}) copy-start(f32[4608]{0:T(1024)} %param.10) | copy-start | bytes 55300
  272.4 83.0 %copy-start.4 = (bf16[128,4608]{1,0:T(8,128)(2,1)}, bf16[128,4608]{1,0:T(8,128)(2,1)S(1)}, u32[]{:S(2)}) copy-start(bf16[128,4608]{1,0:T(8,128)(2,1)S(1)} %scatter_custom_fusion) | copy-start | bytes 3538948
  272.4 80.8 %copy-start.15 = (f32[4608]{0:T(1024)S(1)}, f32[4608]{0:T(1024)}, u32[]{:S(2)}) copy-start(f32[4608]{0:T(1024)} %param.11) | copy-start | bytes 55300
  355.4 43.2 %copy-start.1 = (bf16[128,4608]{1,0:T(8,128)(2,1)}, bf16[128,4608]{1,0:T(8,128)(2,1)S(1)}, u32[]{:S(2)}) copy-start(bf16[128,4608]{1,0:T(8,128)(2,1)S(1)} %scatter_custom_fusion.1) | copy-start | bytes 3538948
  (11 other events, 13.4 us)
Sparse Core Ops, SparseCore 0:
  9.6 20.1 all-gather.10
  32.5 45.9 all-gather.6
  80.0 16.4 all-gather.8
  98.0 17.4 all-gather.12
  116.9 17.4 all-gather.14
  137.7 66.5 reduce-scatter.6
  207.2 44.7 all-gather.16
  257.6 24.8 reduce-scatter.12
  285.9 65.9 reduce-scatter.8
  354.4 39.6 reduce-scatter.10
where the time goes:
time: 406 us; the launch traced here: 405 us
  waiting for transfers between devices  287 us (71%)
  blocking collectives  53.9 us (13%)
  matrix products  23.6 us (6%)
  between operations  15.2 us (4%)
  local copies, waits for them, and re-layouts  15.1 us (4%)
  other arithmetic  10.5 us (3%)
    reduce_scatter x1, waiting for transfers between devices, body(): lax.psum_scatter((total + contract_cols(d_values, value_cols)).astype(jnp...  67.4 us
    reduce_scatter x1, waiting for transfers between devices, body(): lax.psum_scatter(jnp.dot(attended, out_full, preferred_element_type=jnp.f...  63.6 us
    all_gather x1, waiting for transfers between devices, body(): lax.all_gather(sending, 'seq', axis=0, tiled=True)  48.7 us
    all_gather x1, waiting for transfers between devices, body(): d_mix_all = lax.all_gather(d_mix, 'seq', axis=0, tiled=True)  45.3 us
    psum x1, blocking collectives, body(): grad_gain, grad_router = lax.psum((gain_term, router_term), ('seq', 'fsdp'))  40.8 us
    all_gather x1, waiting for transfers between devices, body(): lax.all_gather(w_value, 'fsdp', axis=0, tiled=True)  16.7 us
    all_gather x1, waiting for transfers between devices, body(): out_full = lax.all_gather(w_out, 'fsdp', axis=1, tiled=True)  16.1 us
    all_gather x1, waiting for transfers between devices, body(): lax.all_gather(w_query, 'fsdp', axis=0, tiled=True)  15.5 us
  transfers between devices with their start and end apart: 10, of which 9 were waited for; matrix products, arithmetic and copies ran while one was open for 7% of the time, Pallas kernels for 0%

commit v1 on v0

v1 whole, which is shorter than its diff:
```python
import functools

import jax
import jax.numpy as jnp
from jax import lax
from jax.experimental import pallas as pl
from jax.experimental.pallas import tpu as pltpu
from jax.sharding import PartitionSpec as P

SOFTCAP = 50.0
QUERY_SCALE = 1.0 / 12.0
EPS = 1e-06
MESH = pl.DeviceIdType.MESH
VMEM_LIMIT = 48 * 1024 * 1024


def contract_rows(left, right):
    return lax.dot_general(
        left, right, (((0,), (0,)), ((), ())), preferred_element_type=jnp.float32
    )


def contract_cols(left, right):
    return lax.dot_general(
        left, right, (((1,), (1,)), ((), ())), preferred_element_type=jnp.float32
    )


def place(axis, size):
    me = lax.axis_index(axis)
    return me, me // 2, lax.rem(me, 2), size // 2


def pair_peers(axis, size):
    me, outer, inner, outers = place(axis, size)
    peers = [{axis: lax.rem(outer + d, outers) * 2 + inner} for d in range(1, outers)]
    peers.append({axis: outer * 2 + 1 - inner})
    return peers


def all_peers(axis, size):
    me = lax.axis_index(axis)
    return [{axis: lax.rem(me + d, size)} for d in range(1, size)]


def meet(peers):
    barrier = pltpu.get_barrier_semaphore()
    for peer in peers:
        pl.semaphore_signal(barrier, inc=1, device_id=peer, device_id_type=MESH)
    pl.semaphore_wait(barrier, len(peers))


def remote(src, dst, send, recv, peer):
    return pltpu.make_async_remote_copy(
        src_ref=src, dst_ref=dst, send_sem=send, recv_sem=recv, device_id=peer, device_id_type=MESH
    )


def gather_start(axis, size, src, dst, sems, own_sem):
    me, outer, inner, outers = place(axis, size)
    own = pltpu.make_async_copy(src, dst.at[me], own_sem)
    first = []
    for d in range(1, outers):
        peer = {axis: lax.rem(outer + d, outers) * 2 + inner}
        first.append(remote(src, dst.at[me], sems.at[0, d], sems.at[1, d], peer))
    partner = {axis: outer * 2 + 1 - inner}
    second = [remote(src, dst.at[me], sems.at[2, 0], sems.at[3, 0], partner)]
    for copy in first + second:
        copy.start()
    own.start()
    return own, first, second


def gather_forward(axis, size, dst, sems, copies):
    me, outer, inner, outers = place(axis, size)
    own, first, second = copies
    partner = {axis: outer * 2 + 1 - inner}
    for d in range(1, outers):
        first[d - 1].wait_recv()
        block = lax.rem(outer + outers - d, outers) * 2 + inner
        copy = remote(dst.at[block], dst.at[block], sems.at[2, d], sems.at[3, d], partner)
        copy.start()
        second.append(copy)


def gather_finish(copies):
    own, first, second = copies
    own.wait()
    for copy in first:
        copy.wait_send()
    for copy in second:
        copy.wait()


def gather_kernel(plan, *refs):
    count = len(plan)
    srcs, dsts = refs[:count], refs[count : 2 * count]
    sems, own_sems = refs[2 * count : 3 * count], refs[3 * count]
    peers = []
    for axis, size in dict(plan).items():
        peers += pair_peers(axis, size)
    meet(peers)
    running = [
        gather_start(axis, size, src, dst, sem, own_sems.at[i])
        for i, ((axis, size), src, dst, sem) in enumerate(zip(plan, srcs, dsts, sems))
    ]
    for (axis, size), dst, sem, copies in zip(plan, dsts, sems, running):
        gather_forward(axis, size, dst, sem, copies)
    for copies in running:
        gather_finish(copies)


def gather(plan, arrays, collective_id):
    return pl.pallas_call(
        functools.partial(gather_kernel, plan),
        out_shape=[
            jax.ShapeDtypeStruct((size,) + a.shape, a.dtype) for (_, size), a in zip(plan, arrays)
        ],
        in_specs=[pl.BlockSpec(memory_space=pl.ANY)] * len(arrays),
        out_specs=[pl.BlockSpec(memory_space=pl.ANY)] * len(arrays),
        scratch_shapes=[pltpu.SemaphoreType.DMA((4, size // 2)) for _, size in plan]
        + [pltpu.SemaphoreType.DMA((len(arrays),))],
        compiler_params=pltpu.CompilerParams(
            collective_id=collective_id, has_side_effects=True, vmem_limit_bytes=VMEM_LIMIT
        ),
        name="gather",
    )(*arrays)


def row_chunks(rows, run):
    if rows <= 32:
        run(slice(None))
        return
    step = next(s for s in (96, 64, 48, 32, 16) if rows % s == 0)

    @pl.loop(0, rows // step)
    def _(i):
        run(pl.ds(pl.multiple_of(i * step, step), step))


def scatter_start(axis, size, part, first_in, sems):
    me, outer, inner, outers = place(axis, size)
    partner = {axis: outer * 2 + 1 - inner}
    first = []
    for d in list(range(1, outers)) + [0]:
        to = lax.rem(outer + d, outers)
        copy = remote(
            part.at[to * 2 + 1 - inner], first_in.at[d], sems.at[0, d], sems.at[1, d], partner
        )
        copy.start()
        first.append((d, copy))
    return first


def scatter_step(axis, size, part, first_in, pair, second_in, sems, d, copy):
    me, outer, inner, outers = place(axis, size)
    to = lax.rem(outer + d, outers)
    copy.wait_recv()
    if d == 0:
        return None

    def run(rows):
        total = part[to * 2 + inner, rows].astype(jnp.float32) + first_in[d, rows].astype(
            jnp.float32
        )
        pair[d, rows] = total.astype(pair.dtype)

    row_chunks(part.shape[1], run)
    out = remote(
        pair.at[d], second_in.at[d], sems.at[2, d], sems.at[3, d], {axis: to * 2 + inner}
    )
    out.start()
    return out


def scatter_finish(axis, size, part, first_in, second_in, first, second, store):
    me, outer, inner, outers = place(axis, size)
    for copy in second:
        copy.wait()

    def run(rows):
        total = part[me, rows].astype(jnp.float32) + first_in[0, rows].astype(jnp.float32)
        for d in range(1, outers):
            total = total + second_in[d, rows].astype(jnp.float32)
        store(rows, total)

    row_chunks(part.shape[1], run)
    for _, copy in first:
        copy.wait_send()


def reduce_kernel(plan, splits, *refs):
    count, outs = len(plan), sum(splits)
    parts, out_refs, scratch = refs[:count], refs[count : count + outs], refs[count + outs :]
    peers = []
    for axis, size in dict(plan).items():
        peers += pair_peers(axis, size)
    meet(peers)
    held = [scratch[4 * i : 4 * i + 4] for i in range(count)]
    firsts = [
        scatter_start(axis, size, part, bufs[0], bufs[3])
        for (axis, size), part, bufs in zip(plan, parts, held)
    ]
    seconds = [[] for _ in plan]
    for turn in range(max(len(f) for f in firsts)):
        for i, (axis, size) in enumerate(plan):
            if turn < len(firsts[i]):
                d, copy = firsts[i][turn]
                first_in, pair, second_in, sems = held[i]
                out = scatter_step(
                    axis, size, parts[i], first_in, pair, second_in, sems, d, copy
                )
                if out is not None:
                    seconds[i].append(out)
    at = 0
    for i, (axis, size) in enumerate(plan):
        mine = out_refs[at : at + splits[i]]
        at += splits[i]

        def store(rows, total, mine=mine):
            width = total.shape[1] // len(mine)
            for j, ref in enumerate(mine):
                ref[rows] = total[:, j * width : (j + 1) * width]

        scatter_finish(
            axis, size, parts[i], held[i][0], held[i][2], firsts[i], seconds[i], store
        )


def reduce(plan, splits, arrays, collective_id):
    outs, scratch = [], []
    for (_, size), split, a in zip(plan, splits, arrays):
        outs += [jax.ShapeDtypeStruct((a.shape[1], a.shape[2] // split), jnp.float32)] * split
        scratch += [pltpu.VMEM((size // 2,) + a.shape[1:], a.dtype)] * 3
        scratch += [pltpu.SemaphoreType.DMA((4, size // 2))]
    return pl.pallas_call(
        functools.partial(reduce_kernel, plan, splits),
        out_shape=outs,
        in_specs=[pl.BlockSpec(memory_space=pltpu.VMEM)] * len(arrays),
        out_specs=[pl.BlockSpec(memory_space=pltpu.VMEM)] * len(outs),
        scratch_shapes=scratch,
        compiler_params=pltpu.CompilerParams(
            collective_id=collective_id, has_side_effects=True, vmem_limit_bytes=VMEM_LIMIT
        ),
        name="reduce",
    )(*arrays)


def exchange(axis, size, src, slots, sems):
    me = lax.axis_index(axis)
    copies = []
    for d in range(1, size):
        copies.append(
            remote(
                src, slots.at[me], sems.at[0, d], sems.at[1, d], {axis: lax.rem(me + d, size)}
            )
        )
    for copy in copies:
        copy.start()
    slots[me] = src[...]
    for copy in copies:
        copy.wait()
    total = slots[0]
    for s in range(1, size):
        total = total + slots[s]
    return total


def total_kernel(n_seq, n_fsdp, x_ref, out_ref, mid, slots_f, slots_s, sems_f, sems_s):
    meet(all_peers("seq", n_seq) + all_peers("fsdp", n_fsdp))
    mid[...] = exchange("fsdp", n_fsdp, x_ref, slots_f, sems_f)
    out_ref[...] = exchange("seq", n_seq, mid, slots_s, sems_s)


def total(n_seq, n_fsdp, x, collective_id):
    return pl.pallas_call(
        functools.partial(total_kernel, n_seq, n_fsdp),
        out_shape=jax.ShapeDtypeStruct(x.shape, x.dtype),
        in_specs=[pl.BlockSpec(memory_space=pltpu.VMEM)],
        out_specs=pl.BlockSpec(memory_space=pltpu.VMEM),
        scratch_shapes=[
            pltpu.VMEM(x.shape, x.dtype),
            pltpu.VMEM((n_fsdp,) + x.shape, x.dtype),
            pltpu.VMEM((n_seq,) + x.shape, x.dtype),
            pltpu.SemaphoreType.DMA((2, n_fsdp)),
            pltpu.SemaphoreType.DMA((2, n_seq)),
        ],
        compiler_params=pltpu.CompilerParams(
            collective_id=collective_id, has_side_effects=True, vmem_limit_bytes=VMEM_LIMIT
        ),
        name="total",
    )(x)


def body(
    n_seq, n_fsdp, tokens, norm_gain, router_weight, w_query, w_key, w_value, w_out, cotangent,
    kept_index
):
    own_rows, width = tokens.shape[1], tokens.shape[2]
    slot_list = kept_index[0, 0]
    cap = slot_list.shape[0]
    head_width = w_query.shape[1]
    slots = n_seq * cap
    is_kept = slot_list >= 0
    picked = jnp.where(is_kept, slot_list, 0)
    kept_rows = jnp.where(is_kept[:, None], tokens[0][picked], jnp.zeros((), jnp.bfloat16))
    kept_float = kept_rows.astype(jnp.float32)
    inv_root = lax.rsqrt(jnp.mean(kept_float * kept_float, axis=1) + EPS)
    unit = kept_float * inv_root[:, None]
    sending = (unit * norm_gain).astype(jnp.bfloat16)
    flags = jnp.zeros((128,), jnp.float32).at[:cap].set(is_kept.astype(jnp.float32))
    flags = jnp.broadcast_to(flags[None, :], (8, 128))
    seq, fsdp = ("seq", n_seq), ("fsdp", n_fsdp)
    rows_g, flags_g, query_g, key_g, value_g, out_g = gather(
        (seq, seq, fsdp, fsdp, fsdp, fsdp),
        (sending, flags, w_query, w_key, w_value, w_out),
        1,
    )
    all_rows = rows_g.reshape(slots, width)
    live = flags_g[:, 0, :cap].reshape(slots) > 0.5
    query_cols = query_g.reshape(width, head_width)
    key_cols = key_g.reshape(width, head_width)
    value_cols = value_g.reshape(width, head_width)
    out_full = jnp.swapaxes(out_g, 0, 1).reshape(head_width, width)
    queries = jnp.dot(all_rows, query_cols, preferred_element_type=jnp.float32).astype(jnp.bfloat16)
    keys_all = jnp.dot(all_rows, key_cols, preferred_element_type=jnp.float32).astype(jnp.bfloat16)
    values_all = jnp.dot(all_rows, value_cols, preferred_element_type=jnp.float32).astype(
        jnp.bfloat16
    )
    raw_scores = contract_cols(queries, keys_all) * QUERY_SCALE
    capped = SOFTCAP * jnp.tanh(raw_scores / SOFTCAP)
    order = jnp.arange(slots, dtype=jnp.int32)
    allowed = live[None, :] & ((order[None, :] <= order[:, None]) | ~live[:, None])
    powers = jnp.where(allowed, jnp.exp(capped), 0.0)
    softmax_values = powers / jnp.sum(powers, axis=1, keepdims=True)
    rounded_weights = softmax_values.astype(jnp.bfloat16)
    attended = jnp.dot(rounded_weights, values_all, preferred_element_type=jnp.float32).astype(
        jnp.bfloat16
    )
    (mixed_sum,) = reduce(
        (seq,),
        (1,),
        (
            jnp.dot(attended, out_full, preferred_element_type=jnp.float32)
            .astype(jnp.bfloat16)
            .reshape(n_seq, cap, width),
        ),
        2,
    )
    logits = jnp.dot(kept_float, router_weight, precision=lax.Precision.HIGHEST)
    gate_value = jax.nn.sigmoid(logits)
    cot_rows = jnp.where(
        is_kept[:, None], cotangent[0][picked], jnp.zeros((), jnp.bfloat16)
    ).astype(jnp.float32)
    d_mix = (gate_value[:, None] * cot_rows).astype(jnp.bfloat16)
    (d_mix_g,) = gather((seq,), (d_mix,), 3)
    d_mix_all = d_mix_g.reshape(slots, width)
    new_rows = (kept_float + gate_value[:, None] * mixed_sum).astype(jnp.bfloat16)
    target = jnp.where(is_kept, slot_list, own_rows)
    mixed_rows = tokens[0].at[target].set(new_rows, mode="drop")[None]
    d_gate = jnp.sum(cot_rows * mixed_sum, axis=1)
    d_logit = d_gate * gate_value * (1.0 - gate_value)
    out_part = contract_rows(attended, d_mix_all).astype(jnp.bfloat16)
    out_part = jnp.swapaxes(out_part.reshape(head_width, n_fsdp, width // n_fsdp), 0, 1)
    d_attended = contract_cols(d_mix_all, out_full).astype(jnp.bfloat16)
    d_values = contract_rows(rounded_weights, d_attended).astype(jnp.bfloat16)
    d_probs = contract_cols(d_attended, values_all)
    d_soft = softmax_values * (d_probs - jnp.sum(softmax_values * d_probs, axis=1, keepdims=True))
    d_raw = (d_soft * (1.0 - capped / SOFTCAP * (capped / SOFTCAP)) * QUERY_SCALE).astype(
        jnp.bfloat16
    )
    d_queries = jnp.dot(d_raw, keys_all, preferred_element_type=jnp.float32).astype(jnp.bfloat16)
    d_keys = contract_rows(d_raw, queries).astype(jnp.bfloat16)
    d_stack = jnp.concatenate([d_queries, d_keys, d_values], axis=1)
    stack_part = (
        contract_rows(all_rows, d_stack)
        .astype(jnp.bfloat16)
        .reshape(n_fsdp, width // n_fsdp, 3 * head_width)
    )
    total_in = contract_cols(d_queries, query_cols)
    total_in = total_in + contract_cols(d_keys, key_cols)
    normed_part = (
        (total_in + contract_cols(d_values, value_cols))
        .astype(jnp.bfloat16)
        .reshape(n_seq, cap, width)
    )
    d_normed, grad_query, grad_key, grad_value, out_grad = reduce(
        (seq, fsdp, fsdp), (1, 3, 1), (normed_part, stack_part, out_part), 4
    )
    gain_term = jnp.sum(d_normed * unit, axis=0)
    router_term = jnp.sum(d_logit[:, None] * kept_float, axis=0)
    sums = total(
        n_seq, n_fsdp, jnp.concatenate([gain_term, router_term]).reshape(2 * width // 128, 128), 5
    ).reshape(2 * width)
    grad_gain, grad_router = sums[:width], sums[width:]
    scaled = d_normed * norm_gain
    d_kept = inv_root[:, None] * (scaled - unit * jnp.mean(scaled * unit, axis=1, keepdims=True))
    grad_new = (cot_rows + d_kept + d_logit[:, None] * router_weight).astype(jnp.bfloat16)
    grad_tokens = cotangent[0].at[target].set(grad_new, mode="drop")[None]
    return (
        mixed_rows,
        grad_tokens,
        grad_query,
        grad_key,
        grad_value,
        out_grad,
        grad_gain,
        grad_router,
    )


def solution(mesh):
    in_specs = (
        P("fsdp", "seq", None),
        P(),
        P(),
        P("fsdp", "seq"),
        P("fsdp", "seq"),
        P("fsdp", "seq"),
        P("seq", "fsdp"),
        P("fsdp", "seq", None),
        P("fsdp", "seq", None),
    )
    out_specs = (
        P("fsdp", "seq", None),
        P("fsdp", "seq", None),
        P("fsdp", "seq"),
        P("fsdp", "seq"),
        P("fsdp", "seq"),
        P("seq", "fsdp"),
        P(),
        P(),
    )
    local = functools.partial(body, mesh.shape["seq"], mesh.shape["fsdp"])
    return jax.shard_map(
        local, mesh=mesh, in_specs=in_specs, out_specs=out_specs, check_vma=False
    )
```

time: 406 us -> 189 us (0.47)
  waiting for transfers between devices: 287 us -> 0 us
  Pallas kernels: 0 us -> 141 us
  blocking collectives: 53.9 us -> 0 us
  between operations: 15.2 us -> 1.02 us
  matrix products: 23.6 us -> 15.1 us
  local copies, waits for them, and re-layouts: 15.1 us -> 22.6 us
    all_gather x6 -> x0, waiting for transfers between devices: 144 us -> none  [the longest x1 48.7 us: body(): lax.all_gather(sending, 'seq', axis=0, tiled=True)]
    pallas_call x0 -> x5, Pallas kernels: none -> 141 us  [the longest x2 64.3 us: reduce(): pl.pallas_call(functools.partial(reduce_kernel, plan, splits), out_shape=...]
    reduce_scatter x3 -> x0, waiting for transfers between devices: 131 us -> none  [the longest x1 67.4 us: body(): lax.psum_scatter((total + contract_cols(d_values, value_cols)).astype(jnp...]
    psum x1 -> x0, blocking collectives: 40.8 us -> none  [body(): grad_gain, grad_router = lax.psum((gain_term, router_term), ('seq', 'fsdp'))]
    unnamed x1 -> x0, blocking collectives: 13.1 us -> none
    unnamed x11 -> x0, waiting for transfers between devices: 11.8 us -> none
    unnamed x57 -> x63, local copies, waits for them, and re-layouts: 11.4 us -> 13.4 us
  transfers between devices with their start and end apart: 10 -> 0, of which waited for: 9 -> 0; matrix products, arithmetic and copies ran while one was open for 7% -> 0% of each run, Pallas kernels for 0% -> 0%
where the time goes in v1:
time: 189 us
  Pallas kernels  141 us (75%)
  local copies, waits for them, and re-layouts  22.6 us (12%)
  matrix products  15.1 us (8%)
  other arithmetic  8.92 us (5%)
    pallas_call x2, Pallas kernels, reduce(): pl.pallas_call(functools.partial(reduce_kernel, plan, splits), out_shape=...  64.3 us
    pallas_call x2, Pallas kernels, gather(): pl.pallas_call(functools.partial(gather_kernel, plan), out_shape=[jax.Sha...  63.2 us
    pallas_call x1, Pallas kernels, total(): pl.pallas_call(functools.partial(total_kernel, n_seq, n_fsdp), out_shape=...  13.8 us
    unnamed x63, local copies, waits for them, and re-layouts  13.4 us
    scatter x1, other arithmetic, body(): grad_tokens = cotangent[0].at[target].set(grad_new, mode='drop')[None]  4.15 us
    dot_general x4, matrix products, contract_rows(): lax.dot_general(left, right, (((0,), (0,)), ((), ())), preferred_element_...  4.06 us

profile of v1, /device:TPU:0, one launch (start us, length us, event | category | flops | bytes accessed | tf_op | source)
XLA Modules:
  0.0 188.9 jit_solution(12561744558676211168)
XLA Ops:
  0.6 1.4 copy.28
  2.3 1.0 copy.29
  5.1 34.1 %gather.14 = (bf16[8,24,4608]{2,1,0:T(8,128)(2,1)}, f32[8,8,128]{2,1,0:T(8,128)S(1)}, bf16[4,1152,128]{2,1,0:T(8,128)(2,1)S(1)}, bf16[4,1152,128]{2,1,0:T(8,128)...) custom-call(bf16[24,4608]{1,0:T(8,128)(2,1)S(1)} %fusion.14.refs_0_, ...), custom_call_target="tpu_custom_call" | custom-call | tf_op jit(solution)/shard_map/gather/pallas_call | solution.py:114
  39.2 1.0 copy-done
  40.2 1.0 copy-done.2
  41.3 2.1 %convolution_convert_fusion.8 = bf16[192,128]{1,0:T(8,128)(2,1)S(1)} fusion(bf16[192,4608]{1,0:T(8,128)(2,1)} %bitcast.83, bf16[4608,128]{1,0:T(8,128)(2,1)S(1)} %bitcast.76), kind=kOutput, calls=%fused_computation.17 | convolution fusion | flops 226516992 | bytes 2998272 | tf_op jit(solution)/shard_map/dot_general | solution.py:327
  43.5 2.5 %convolution_convert_fusion.10 = bf16[192,128]{1,0:T(8,128)(2,1)S(1)} fusion(bf16[192,4608]{1,0:T(8,128)(2,1)} %bitcast.84, bf16[4608,128]{1,0:T(8,128)(2,1)} %bitcast.80), kind=kOutput, calls=%fused_computation.19 | convolution fusion | flops 226516992 | bytes 2998272 | tf_op jit(solution)/shard_map/dot_general | solution.py:325
  47.2 2.4 %copy.17 = bf16[128,4,1152]{0,2,1:T(8,128)(2,1)} copy(bf16[128,4,1152]{2,0,1:T(8,128)(2,1)} %bitcast.82) | data formatting | bytes 2359296 | tf_op jit(solution)/shard_map/transpose | solution.py:324
  49.6 1.9 %convolution_convert_fusion.1 = bf16[192,4608]{1,0:T(8,128)(2,1)S(1)} fusion(bf16[192,128]{1,0:T(8,128)(2,1)S(1)} %convolution_convert_fusion.7, bf16[128,4608]{0,1:T(8,128)(2,1)} %bitcast.88), kind=kOutput, calls=%fused_computation.8 | convolution fusion | flops 227377152 | bytes 2998272 | tf_op jit(solution)/shard_map/dot_general | solution.py:344
  51.6 27.8 %reduce.6 = f32[24,4608]{1,0:T(8,128)S(1)} custom-call(bf16[8,24,4608]{2,1,0:T(8,128)(2,1)S(1)} %bitcast.74), custom_call_target="tpu_custom_call" | custom-call | tf_op jit(solution)/shard_map/reduce/pallas_call | solution.py:236
  79.8 3.5 %scatter_custom_fusion = bf16[128,4608]{1,0:T(8,128)(2,1)} fusion(bf16[128,4608]{1,0:T(8,128)(2,1)} %bitcast.94, s32[24]{0:T(128)S(1)} %get-tuple-element.50, f32[24,4608]{1,0:T(8,128)S(1)} %reduce.6, f32[24]{0:T(128)S(1)} %fusion.5, bf16[24,4608]{1,0:T(8,128)(2,1)S(1)} %copy-done.19, pred[24]{0:T(512)(128)(4,1)S(1)} %compare_bitcast_fusion), kind=kCustom, calls=%fused_computation.48 | custom fusion | flops 552960 | bytes 1844224 | tf_op jit(solution)/shard_map/scatter | solution.py:360
  83.2 2.3 %gather_fusion.1 = bf16[24,4608]{1,0:T(8,128)(2,1)S(1)} fusion(bf16[128,4608]{1,0:T(8,128)(2,1)} %bitcast.90, s32[1024]{0:T(1024)S(1)} %pad_clamp_fusion), kind=kCustom, calls=%fused_computation.1 | custom fusion | bytes 442464 | tf_op jit(solution)/shard_map/gather | solution.py:353
  85.9 29.0 %gather.15 = bf16[8,24,4608]{2,1,0:T(8,128)(2,1)S(1)} custom-call(bf16[24,4608]{1,0:T(8,128)(2,1)S(1)} %get-tuple-element.46.refs_0_), custom_call_target="tpu_custom_call" | custom-call | tf_op jit(solution)/shard_map/gather/pallas_call | solution.py:114
  119.1 0.8 copy-done.16
  120.0 3.2 %convolution_convert_fusion = bf16[4608,384]{1,0:T(8,128)(2,1)} fusion(bf16[192,4608]{1,0:T(8,128)(2,1)S(1)} %bitcast.86, bf16[192,128]{1,0:T(8,128)(2,1)S(1)} %convolution_convert_fusion.3, bf16[192,128]{1,0:T(8,128)(2,1)S(1)} %convolution_convert_fusion.4, bf16[192,128]{1,0:T(8,128)(2,1)S(1)} %convolution_convert_fusion.5), kind=kOutput, calls=%fused_computation.4 | convolution fusion | flops 681689088 | bytes 5455872 | tf_op jit(solution)/shard_map/dot_general | solution.py:18
  123.7 1.4 copy.18
  125.1 1.7 copy.19
  126.8 36.5 %reduce.7 = (f32[24,4608]{1,0:T(8,128)S(1)}, f32[1152,128]{1,0:T(8,128)S(1)}, f32[1152,128]{1,0:T(8,128)S(1)}, f32[1152,128]{1,0:T(8,128)S(1)}, f32[128,1152]{1,0:T(8,128)S(1)}) custom-call(bf16[8,24,4608]{2,1,0:T(8,128)(2,1)S(1)} %bitcast.73, bf16[4,1152,384]{2,1,0:T(8,128)(2,1)} %bitcast.87, bf16[4,128,1152]{2,1,0:T(8,128)(2,1)S(1)} %bitcast.75), custom_call_target="tpu_custom_call" | custom-call | tf_op jit(solution)/shard_map/reduce/pallas_call | solution.py:236
  164.2 0.8 copy-done.5
  167.0 4.2 %scatter_custom_fusion.1 = bf16[128,4608]{1,0:T(8,128)(2,1)} fusion(bf16[128,4608]{1,0:T(8,128)(2,1)} %bitcast.91, s32[24]{0:T(128)S(1)} %get-tuple-element.50, f32[24,4608]{1,0:T(8,128)S(1)} %get-tuple-element.37, f32[4608]{0:T(1024)S(1)} %copy-done.26, f32[24]{0:T(128)S(1)} %subtract_multiply_fusion, f32[24]{0:T(128)S(1)} %broadcast_multiply_fusion, ...), kind=kCustom, calls=%fused_computation.49 | custom fusion | flops 1437696 | bytes 2107392 | tf_op jit(solution)/shard_map/scatter | solution.py:399
  171.2 13.8 %total.1 = f32[72,128]{1,0:T(8,128)S(1)} custom-call(f32[72,128]{1,0:T(8,128)S(1)} %pad_maximum_fusion.x_ref), custom_call_target="tpu_custom_call" | custom-call | tf_op jit(solution)/shard_map/total/pallas_call | solution.py:276
  185.6 0.8 copy.30
  186.5 0.8 copy.31
  187.3 0.8 copy.32
  (86 shorter events, 12.9 us)
Async XLA Ops:
  0.6 1.6 copy-start.23
  2.3 1.4 copy-start.21
  2.3 1.0 copy-start.27
  3.3 1.4 copy-start.24
  3.7 1.4 copy-start.11
  3.7 1.4 copy-start.12
  3.7 1.4 copy-start.13
  3.7 1.4 copy-start.14
  39.2 1.0 copy-start
  40.2 1.0 copy-start.2
  43.5 2.6 %copy-start.15 = (bf16[8,24,4608]{2,1,0:T(8,128)(2,1)S(1)}, bf16[8,24,4608]{2,1,0:T(8,128)(2,1)}, u32[]{:S(2)}) copy-start(bf16[8,24,4608]{2,1,0:T(8,128)(2,1)} %get-tuple-element.32) | copy-start | bytes 5308420
  51.5 27.8 %copy-start.26 = (f32[4608]{0:T(1024)S(1)}, f32[4608]{0:T(1024)}, u32[]{:S(2)}) copy-start(f32[4608]{0:T(1024)} %param.13) | copy-start | bytes 55300
  51.5 27.9 %copy-start.19 = (bf16[24,4608]{1,0:T(8,128)(2,1)S(1)}, bf16[24,4608]{1,0:T(8,128)(2,1)}, u32[]{:S(2)}) copy-start(bf16[24,4608]{1,0:T(8,128)(2,1)} %copy-done.18) | copy-start | bytes 663556
  85.6 29.3 %copy-start.22 = (bf16[24,4608]{1,0:T(8,128)(2,1)}, bf16[24,4608]{1,0:T(8,128)(2,1)S(1)}, u32[]{:S(2)}) copy-start(bf16[24,4608]{1,0:T(8,128)(2,1)S(1)} %gather_fusion.1) | copy-start | bytes 663556
  85.9 29.1 %copy-start.17 = (bf16[128,4,1152]{0,2,1:T(8,128)(2,1)S(1)}, bf16[128,4,1152]{0,2,1:T(8,128)(2,1)}, u32[]{:S(2)}) copy-start(bf16[128,4,1152]{0,2,1:T(8,128)(2,1)} %copy.17) | copy-start | bytes 3538948
  115.5 1.3 copy-start.1
  118.5 1.5 copy-start.16
  126.8 39.9 %copy-start.20 = (bf16[24,4608]{1,0:T(8,128)(2,1)S(1)}, bf16[24,4608]{1,0:T(8,128)(2,1)}, u32[]{:S(2)}) copy-start(bf16[24,4608]{1,0:T(8,128)(2,1)} %copy-done.18) | copy-start | bytes 663556
  126.8 39.8 %copy-start.25 = (f32[4608]{0:T(1024)S(1)}, f32[4608]{0:T(1024)}, u32[]{:S(2)}) copy-start(f32[4608]{0:T(1024)} %param.12) | copy-start | bytes 55300
  163.3 0.8 copy-start.3
  167.0 18.6 %copy-start.10 = (f32[1152,128]{1,0:T(8,128)S(1)}, f32[1152,128]{1,0:T(8,128)}, u32[]{:S(2)}) copy-start(f32[1152,128]{1,0:T(8,128)} %copy-done.9) | copy-start | bytes 1769476
  171.2 15.3 %copy-start.8 = (f32[1152,128]{1,0:T(8,128)S(1)}, f32[1152,128]{1,0:T(8,128)}, u32[]{:S(2)}) copy-start(f32[1152,128]{1,0:T(8,128)} %copy-done.7) | copy-start | bytes 1769476
  185.6 1.6 copy-start.6
  186.5 1.6 copy-start.4
  (4 other events, 3.1 us)

commit v2 on v1

--- a/solution.py
+++ b/solution.py
@@ -56,69 +56,79 @@
     )
 
 
-def gather_start(axis, size, src, dst, sems, own_sem):
-    me, outer, inner, outers = place(axis, size)
-    own = pltpu.make_async_copy(src, dst.at[me], own_sem)
+def piece(ref, index, chunks, c):
+    if chunks == 1:
+        return ref.at[index]
+    step = ref.shape[2] // chunks
+    return ref.at[index, :, pl.ds(c * step, step)]
+
+
+def gather_start(axis, size, src, dst, sems, chunks, c):
+    me, outer, inner, outers = place(axis, size)
+    step = src.shape[1] // chunks
+    block = src if chunks == 1 else src.at[:, pl.ds(c * step, step)]
+    land = piece(dst, me, chunks, c)
     first = []
     for d in range(1, outers):
         peer = {axis: lax.rem(outer + d, outers) * 2 + inner}
-        first.append(remote(src, dst.at[me], sems.at[0, d], sems.at[1, d], peer))
+        first.append(remote(block, land, sems.at[0, d, c], sems.at[1, d, c], peer))
     partner = {axis: outer * 2 + 1 - inner}
-    second = [remote(src, dst.at[me], sems.at[2, 0], sems.at[3, 0], partner)]
+    second = [remote(block, land, sems.at[2, 0, c], sems.at[3, 0, c], partner)]
     for copy in first + second:
         copy.start()
-    own.start()
-    return own, first, second
-
-
-def gather_forward(axis, size, dst, sems, copies):
-    me, outer, inner, outers = place(axis, size)
-    own, first, second = copies
+    return first, second
+
+
+def gather_forward(axis, size, dst, sems, copies, chunks, c):
+    me, outer, inner, outers = place(axis, size)
+    first, second = copies
     partner = {axis: outer * 2 + 1 - inner}
     for d in range(1, outers):
         first[d - 1].wait_recv()
-        block = lax.rem(outer + outers - d, outers) * 2 + inner
-        copy = remote(dst.at[block], dst.at[block], sems.at[2, d], sems.at[3, d], partner)
+        land = piece(dst, lax.rem(outer + outers - d, outers) * 2 + inner, chunks, c)
+        copy = remote(land, land, sems.at[2, d, c], sems.at[3, d, c], partner)
         copy.start()
         second.append(copy)
 
 
-def gather_finish(copies):
-    own, first, second = copies
-    own.wait()
-    for copy in first:
-        copy.wait_send()
-    for copy in second:
-        copy.wait()
-
-
-def gather_kernel(plan, *refs):
+def gather_kernel(plan, order, *refs):
     count = len(plan)
     srcs, dsts = refs[:count], refs[count : 2 * count]
     sems, own_sems = refs[2 * count : 3 * count], refs[3 * count]
     peers = []
-    for axis, size in dict(plan).items():
+    for axis, size in dict(p[:2] for p in plan).items():
         peers += pair_peers(axis, size)
     meet(peers)
-    running = [
-        gather_start(axis, size, src, dst, sem, own_sems.at[i])
-        for i, ((axis, size), src, dst, sem) in enumerate(zip(plan, srcs, dsts, sems))
-    ]
-    for (axis, size), dst, sem, copies in zip(plan, dsts, sems, running):
-        gather_forward(axis, size, dst, sem, copies)
-    for copies in running:
-        gather_finish(copies)
-
-
-def gather(plan, arrays, collective_id):
+    running = []
+    for i, c in order:
+        axis, size, chunks = plan[i]
+        running.append(gather_start(axis, size, srcs[i], dsts[i], sems[i], chunks, c))
+    owns = []
+    for i, (axis, size, _) in enumerate(plan):
+        own = pltpu.make_async_copy(srcs[i], dsts[i].at[lax.axis_index(axis)], own_sems.at[i])
+        own.start()
+        owns.append(own)
+    for (i, c), copies in zip(order, running):
+        axis, size, chunks = plan[i]
+        gather_forward(axis, size, dsts[i], sems[i], copies, chunks, c)
+    for first, second in running:
+        for copy in first:
+            copy.wait_send()
+        for copy in second:
+            copy.wait()
+    for own in owns:
+        own.wait()
+
+
+def gather(plan, order, arrays, collective_id):
     return pl.pallas_call(
-        functools.partial(gather_kernel, plan),
+        functools.partial(gather_kernel, plan, order),
         out_shape=[
-            jax.ShapeDtypeStruct((size,) + a.shape, a.dtype) for (_, size), a in zip(plan, arrays)
+            jax.ShapeDtypeStruct((p[1],) + a.shape, a.dtype) for p, a in zip(plan, arrays)
         ],
         in_specs=[pl.BlockSpec(memory_space=pl.ANY)] * len(arrays),
         out_specs=[pl.BlockSpec(memory_space=pl.ANY)] * len(arrays),
-        scratch_shapes=[pltpu.SemaphoreType.DMA((4, size // 2)) for _, size in plan]
+        scratch_shapes=[pltpu.SemaphoreType.DMA((4, size // 2, chunks)) for _, size, chunks in plan]
         + [pltpu.SemaphoreType.DMA((len(arrays),))],
         compiler_params=pltpu.CompilerParams(
             collective_id=collective_id, has_side_effects=True, vmem_limit_bytes=VMEM_LIMIT
@@ -138,18 +148,18 @@
         run(pl.ds(pl.multiple_of(i * step, step), step))
 
 
-def scatter_start(axis, size, part, first_in, sems):
-    me, outer, inner, outers = place(axis, size)
-    partner = {axis: outer * 2 + 1 - inner}
-    first = []
-    for d in list(range(1, outers)) + [0]:
-        to = lax.rem(outer + d, outers)
-        copy = remote(
-            part.at[to * 2 + 1 - inner], first_in.at[d], sems.at[0, d], sems.at[1, d], partner
-        )
-        copy.start()
-        first.append((d, copy))
-    return first
+def scatter_start(axis, size, part, first_in, sems, d):
+    me, outer, inner, outers = place(axis, size)
+    to = lax.rem(outer + d, outers)
+    copy = remote(
+        part.at[to * 2 + 1 - inner],
+        first_in.at[d],
+        sems.at[0, d],
+        sems.at[1, d],
+        {axis: outer * 2 + 1 - inner},
+    )
+    copy.start()
+    return copy
 
 
 def scatter_step(axis, size, part, first_in, pair, second_in, sems, d, copy):
@@ -197,21 +207,23 @@
         peers += pair_peers(axis, size)
     meet(peers)
     held = [scratch[4 * i : 4 * i + 4] for i in range(count)]
-    firsts = [
-        scatter_start(axis, size, part, bufs[0], bufs[3])
-        for (axis, size), part, bufs in zip(plan, parts, held)
-    ]
-    seconds = [[] for _ in plan]
-    for turn in range(max(len(f) for f in firsts)):
-        for i, (axis, size) in enumerate(plan):
-            if turn < len(firsts[i]):
-                d, copy = firsts[i][turn]
-                first_in, pair, second_in, sems = held[i]
-                out = scatter_step(
-                    axis, size, parts[i], first_in, pair, second_in, sems, d, copy
-                )
-                if out is not None:
-                    seconds[i].append(out)
+    order = []
+    for d in range(1, max(size for _, size in plan) // 2):
+        order += [(i, d) for i, (_, size) in enumerate(plan) if d < size // 2]
+    order += [(i, 0) for i in range(count)]
+    firsts, seconds = [[] for _ in plan], [[] for _ in plan]
+    sent = []
+    for i, d in order:
+        axis, size = plan[i]
+        copy = scatter_start(axis, size, parts[i], held[i][0], held[i][3], d)
+        firsts[i].append((d, copy))
+        sent.append(copy)
+    for (i, d), copy in zip(order, sent):
+        axis, size = plan[i]
+        first_in, pair, second_in, sems = held[i]
+        out = scatter_step(axis, size, parts[i], first_in, pair, second_in, sems, d, copy)
+        if out is not None:
+            seconds[i].append(out)
     at = 0
     for i, (axis, size) in enumerate(plan):
         mine = out_refs[at : at + splits[i]]
@@ -310,12 +322,22 @@
     sending = (unit * norm_gain).astype(jnp.bfloat16)
     flags = jnp.zeros((128,), jnp.float32).at[:cap].set(is_kept.astype(jnp.float32))
     flags = jnp.broadcast_to(flags[None, :], (8, 128))
+    logits = jnp.dot(kept_float, router_weight, precision=lax.Precision.HIGHEST)
+    gate_value = jax.nn.sigmoid(logits)
+    cot_rows = jnp.where(
+        is_kept[:, None], cotangent[0][picked], jnp.zeros((), jnp.bfloat16)
+    ).astype(jnp.float32)
+    d_mix = (gate_value[:, None] * cot_rows).astype(jnp.bfloat16)
     seq, fsdp = ("seq", n_seq), ("fsdp", n_fsdp)
-    rows_g, flags_g, query_g, key_g, value_g, out_g = gather(
-        (seq, seq, fsdp, fsdp, fsdp, fsdp),
-        (sending, flags, w_query, w_key, w_value, w_out),
+    rows_g, flags_g, query_g, key_g, value_g, out_g, d_mix_g = gather(
+        (seq + (3,), seq + (1,), fsdp + (1,), fsdp + (1,), fsdp + (1,), fsdp + (1,), seq + (3,)),
+        (
+            (1, 0), (0, 0), (2, 0), (0, 1), (3, 0), (0, 2), (4, 0), (6, 0), (5, 0), (6, 1), (6, 2)
+        ),
+        (sending, flags, w_query, w_key, w_value, w_out, d_mix),
         1,
     )
+    d_mix_all = d_mix_g.reshape(slots, width)
     all_rows = rows_g.reshape(slots, width)
     live = flags_g[:, 0, :cap].reshape(slots) > 0.5
     query_cols = query_g.reshape(width, head_width)
@@ -337,29 +359,11 @@
     attended = jnp.dot(rounded_weights, values_all, preferred_element_type=jnp.float32).astype(
         jnp.bfloat16
     )
-    (mixed_sum,) = reduce(
-        (seq,),
-        (1,),
-        (
-            jnp.dot(attended, out_full, preferred_element_type=jnp.float32)
-            .astype(jnp.bfloat16)
-            .reshape(n_seq, cap, width),
-        ),
-        2,
-    )
-    logits = jnp.dot(kept_float, router_weight, precision=lax.Precision.HIGHEST)
-    gate_value = jax.nn.sigmoid(logits)
-    cot_rows = jnp.where(
-        is_kept[:, None], cotangent[0][picked], jnp.zeros((), jnp.bfloat16)
-    ).astype(jnp.float32)
-    d_mix = (gate_value[:, None] * cot_rows).astype(jnp.bfloat16)
-    (d_mix_g,) = gather((seq,), (d_mix,), 3)
-    d_mix_all = d_mix_g.reshape(slots, width)
-    new_rows = (kept_float + gate_value[:, None] * mixed_sum).astype(jnp.bfloat16)
-    target = jnp.where(is_kept, slot_list, own_rows)
-    mixed_rows = tokens[0].at[target].set(new_rows, mode="drop")[None]
-    d_gate = jnp.sum(cot_rows * mixed_sum, axis=1)
-    d_logit = d_gate * gate_value * (1.0 - gate_value)
+    mixed_part = (
+        jnp.dot(attended, out_full, preferred_element_type=jnp.float32)
+        .astype(jnp.bfloat16)
+        .reshape(n_seq, cap, width)
+    )
     out_part = contract_rows(attended, d_mix_all).astype(jnp.bfloat16)
     out_part = jnp.swapaxes(out_part.reshape(head_width, n_fsdp, width // n_fsdp), 0, 1)
     d_attended = contract_cols(d_mix_all, out_full).astype(jnp.bfloat16)
@@ -384,13 +388,21 @@
         .astype(jnp.bfloat16)
         .reshape(n_seq, cap, width)
     )
-    d_normed, grad_query, grad_key, grad_value, out_grad = reduce(
-        (seq, fsdp, fsdp), (1, 3, 1), (normed_part, stack_part, out_part), 4
-    )
+    mixed_sum, d_normed, grad_query, grad_key, grad_value, out_grad = reduce(
+        (seq, seq, fsdp, fsdp),
+        (1, 1, 3, 1),
+        (mixed_part, normed_part, stack_part, out_part),
+        2,
+    )
+    new_rows = (kept_float + gate_value[:, None] * mixed_sum).astype(jnp.bfloat16)
+    target = jnp.where(is_kept, slot_list, own_rows)
+    mixed_rows = tokens[0].at[target].set(new_rows, mode="drop")[None]
+    d_gate = jnp.sum(cot_rows * mixed_sum, axis=1)
+    d_logit = d_gate * gate_value * (1.0 - gate_value)
     gain_term = jnp.sum(d_normed * unit, axis=0)
     router_term = jnp.sum(d_logit[:, None] * kept_float, axis=0)
     sums = total(
-        n_seq, n_fsdp, jnp.concatenate([gain_term, router_term]).reshape(2 * width // 128, 128), 5
+        n_seq, n_fsdp, jnp.concatenate([gain_term, router_term]).reshape(2 * width // 128, 128), 3
     ).reshape(2 * width)
     grad_gain, grad_router = sums[:width], sums[width:]
     scaled = d_normed * norm_gain

time: 189 us -> 168 us (0.89)
  Pallas kernels: 141 us -> 119 us
  matrix products: 15.1 us -> 17.6 us
  local copies, waits for them, and re-layouts: 22.6 us -> 20.5 us
    pallas_call x2 -> x1, Pallas kernels: 64.3 us -> 50.4 us  [reduce(): pl.pallas_call(functools.partial(reduce_kernel, plan, splits), out_shape=...]
    pallas_call x2 -> x1, Pallas kernels: 63.2 us -> 53.2 us  [gather(): pl.pallas_call(functools.partial(gather_kernel, plan, order), out_shape=[...]
    scatter x1, other arithmetic: 4.15 us -> 1.93 us  [body(): grad_tokens = cotangent[0].at[target].set(grad_new, mode='drop')[None]]
    unnamed x63 -> x89, local copies, waits for them, and re-layouts: 13.4 us -> 13.4 us
where the time goes in v2:
time: 168 us; the launch traced here: 167 us
  Pallas kernels  119 us (71%)
  local copies, waits for them, and re-layouts  20.5 us (12%)
  matrix products  17.6 us (10%)
  other arithmetic  8.66 us (5%)
    pallas_call x1, Pallas kernels, gather(): pl.pallas_call(functools.partial(gather_kernel, plan, order), out_shape=[...  53.2 us
    pallas_call x1, Pallas kernels, reduce(): pl.pallas_call(functools.partial(reduce_kernel, plan, splits), out_shape=...  50.4 us
    pallas_call x1, Pallas kernels, total(): pl.pallas_call(functools.partial(total_kernel, n_seq, n_fsdp), out_shape=...  15.6 us
    unnamed x89, local copies, waits for them, and re-layouts  13.4 us
    dot_general x6, matrix products, contract_cols(): lax.dot_general(left, right, (((1,), (1,)), ((), ())), preferred_element_...  4.21 us
    scatter x1, other arithmetic, body(): mixed_rows = tokens[0].at[target].set(new_rows, mode='drop')[None]  4.14 us
    dot_general x4, matrix products, contract_rows(): lax.dot_general(left, right, (((0,), (0,)), ((), ())), preferred_element_...  4.13 us
    dot_general x1, matrix products, body(): jnp.dot(all_rows, value_cols, preferred_element_type=jnp.float32)  3.56 us

profile of v2, /device:TPU:0, one launch (start us, length us, event | category | flops | bytes accessed | tf_op | source)
XLA Modules:
  0.0 167.1 jit_solution(13504366266929224321)
XLA Ops:
  0.6 1.4 copy.28
  6.6 1.0 copy-done.17
  7.6 53.2 %gather.13 = (bf16[8,24,4608]{2,1,0:T(8,128)(2,1)}, f32[8,8,128]{2,1,0:T(8,128)S(1)}, bf16[4,1152,128]{2,1,0:T(8,128)(2,1)S(1)}, bf16[4,1152,128]{2,1,0:T(8,128)...) custom-call(bf16[24,4608]{1,0:T(8,128)(2,1)S(1)} %get-tuple-element.52.ref, ...), custom_call_target="tpu_custom_call" | custom-call | tf_op jit(solution)/shard_map/gather/pallas_call | solution.py:124
  60.8 3.6 %convolution_convert_fusion.8 = bf16[192,128]{1,0:T(8,128)(2,1)} fusion(bf16[192,4608]{1,0:T(8,128)(2,1)} %bitcast.79, bf16[4608,128]{1,0:T(8,128)(2,1)S(1)} %bitcast.72), kind=kOutput, calls=%fused_computation.17 | convolution fusion | flops 226516992 | bytes 2998272 | tf_op jit(solution)/shard_map/dot_general | solution.py:349
  65.6 2.2 %convolution_convert_fusion.10 = bf16[192,128]{1,0:T(8,128)(2,1)S(1)} fusion(bf16[192,4608]{1,0:T(8,128)(2,1)} %bitcast.80, bf16[4608,128]{1,0:T(8,128)(2,1)S(1)} %bitcast.77), kind=kOutput, calls=%fused_computation.19 | convolution fusion | flops 226516992 | bytes 2998272 | tf_op jit(solution)/shard_map/dot_general | solution.py:347
  69.8 1.4 copy.17
  71.2 2.0 %convolution_convert_fusion.1 = bf16[192,4608]{1,0:T(8,128)(2,1)S(1)} fusion(bf16[192,128]{1,0:T(8,128)(2,1)S(1)} %convolution_convert_fusion.7, bf16[128,4608]{0,1:T(8,128)(2,1)} %bitcast.84), kind=kOutput, calls=%fused_computation.8 | convolution fusion | flops 227377152 | bytes 2998272 | tf_op jit(solution)/shard_map/dot_general | solution.py:363
  77.5 1.9 %fusion = bf16[192,4608]{1,0:T(8,128)(2,1)} fusion(f32[192,4608]{1,0:T(8,128)S(1)} %convolution_add_fusion.1, bf16[192,128]{1,0:T(8,128)(2,1)S(1)} %convolution_convert_fusion.3, bf16[4608,128]{1,0:T(8,128)(2,1)S(1)} %bitcast.73), kind=kOutput, calls=%fused_computation.7 | convolution fusion | flops 228261888 | bytes 6537216 | tf_op jit(solution)/shard_map/dot_general | solution.py:24
  79.4 3.3 %convolution_convert_fusion = bf16[4608,384]{1,0:T(8,128)(2,1)} fusion(bf16[192,4608]{1,0:T(8,128)(2,1)S(1)} %bitcast.82, bf16[192,128]{1,0:T(8,128)(2,1)S(1)} %convolution_convert_fusion.3, bf16[192,128]{1,0:T(8,128)(2,1)S(1)} %convolution_convert_fusion.4, bf16[192,128]{1,0:T(8,128)(2,1)S(1)} %convolution_convert_fusion.5), kind=kOutput, calls=%fused_computation.4 | convolution fusion | flops 681689088 | bytes 5455872 | tf_op jit(solution)/shard_map/dot_general | solution.py:18
  83.1 1.4 copy.18
  84.5 1.7 copy.19
  86.2 50.4 %reduce.5 = (f32[24,4608]{1,0:T(8,128)S(1)}, f32[24,4608]{1,0:T(8,128)S(1)}, f32[1152,128]{1,0:T(8,128)S(1)}, f32[1152,128]{1,0:T(8,128)S(1)}, f32[1152,128]{1,0:T(8,128)S(1)}, /*index=5*/f32[128,1152]{1,0:T(8,128)S(1)}) custom-call(bf16[8,24,4608]{2,1,0:T(8,128)(2,1)S(1)} %bitcast.71, bf16[8,24,4608]{2,1,0:T(8,128)(2,1)} %bitcast.94, ...), custom_call_target="tpu_custom_call" | custom-call | tf_op jit(solution)/shard_map/reduce/pallas_call | solution.py:248
  136.6 0.8 copy-done.4
  137.4 0.8 copy-done.6
  138.2 0.8 copy-done.8
  139.0 0.8 copy-done.10
  139.8 0.8 copy-done.12
  140.7 4.1 %scatter_custom_fusion = bf16[128,4608]{1,0:T(8,128)(2,1)} fusion(bf16[128,4608]{1,0:T(8,128)(2,1)} %bitcast.90, s32[24]{0:T(128)} %get-tuple-element.54, f32[24,4608]{1,0:T(8,128)} %copy-done.4, f32[24]{0:T(128)S(1)} %fusion.5, bf16[24,4608]{1,0:T(8,128)(2,1)} %copy-done.21, pred[24]{0:T(512)(128)(4,1)S(1)} %compare_bitcast_fusion), kind=kCustom, calls=%fused_computation.48 | custom fusion | flops 552960 | bytes 1843320 | tf_op jit(solution)/shard_map/scatter | solution.py:399
  145.5 1.9 %scatter_custom_fusion.1 = bf16[128,4608]{1,0:T(8,128)(2,1)S(1)} fusion(bf16[128,4608]{1,0:T(8,128)(2,1)S(1)} %bitcast.87, s32[24]{0:T(128)} %get-tuple-element.54, f32[24,4608]{1,0:T(8,128)S(1)} %get-tuple-element.41, f32[4608]{0:T(1024)S(1)} %copy-done.37, f32[24]{0:T(128)S(1)} %subtract_multiply_fusion, f32[24]{0:T(128)S(1)} %broadcast_multiply_fusion, ...), kind=kCustom, calls=%fused_computation.49 | custom fusion | flops 1437696 | bytes 2107392 | tf_op jit(solution)/shard_map/scatter | solution.py:411
  147.5 15.6 %total.1 = f32[72,128]{1,0:T(8,128)S(1)} custom-call(f32[72,128]{1,0:T(8,128)S(1)} %pad_maximum_fusion.x_ref), custom_call_target="tpu_custom_call" | custom-call | tf_op jit(solution)/shard_map/total/pallas_call | solution.py:288
  163.8 0.8 copy.30
  164.6 0.8 copy.31
  165.4 0.8 copy.32
  166.2 0.8 copy.33
  (110 shorter events, 13.6 us)
Async XLA Ops:
  0.6 1.6 copy-start.30
  2.3 1.3 copy-start.26
  2.3 1.3 copy-start.36
  2.3 2.3 %copy-start.23 = (bf16[1,128,4608]{2,1,0:T(8,128)(2,1)}, bf16[1,128,4608]{2,1,0:T(8,128)(2,1)S(1)}, u32[]{:S(2)}) copy-start(bf16[1,128,4608]{2,1,0:T(8,128)(2,1)S(1)} %copy.29) | copy-start | bytes 3538948
  4.3 1.4 copy-start.21
  60.7 4.9 %copy-start.2 = (bf16[4,1152,128]{2,1,0:T(8,128)(2,1)}, bf16[4,1152,128]{2,1,0:T(8,128)(2,1)S(1)}, u32[]{:S(2)}) copy-start(bf16[4,1152,128]{2,1,0:T(8,128)(2,1)S(1)} %get-tuple-element.35) | copy-start | bytes 3538948
  60.8 7.1 %copy-start = (bf16[4,1152,128]{2,1,0:T(8,128)(2,1)}, bf16[4,1152,128]{2,1,0:T(8,128)(2,1)S(1)}, u32[]{:S(2)}) copy-start(bf16[4,1152,128]{2,1,0:T(8,128)(2,1)S(1)} %get-tuple-element.36) | copy-start | bytes 3538948
  65.6 2.2 %copy-start.18 = (bf16[8,24,4608]{2,1,0:T(8,128)(2,1)S(1)}, bf16[8,24,4608]{2,1,0:T(8,128)(2,1)}, u32[]{:S(2)}) copy-start(bf16[8,24,4608]{2,1,0:T(8,128)(2,1)} %get-tuple-element.34) | copy-start | bytes 5308420
  68.5 1.3 copy-start.31
  71.2 2.1 %copy-start.20 = (bf16[128,4,1152]{0,2,1:T(8,128)(2,1)S(1)}, bf16[128,4,1152]{0,2,1:T(8,128)(2,1)}, u32[]{:S(2)}) copy-start(bf16[128,4,1152]{0,2,1:T(8,128)(2,1)} %copy.17) | copy-start | bytes 3538948
  71.2 2.2 %copy-start.27 = (bf16[8,24,4608]{2,1,0:T(8,128)(2,1)S(1)}, bf16[8,24,4608]{2,1,0:T(8,128)(2,1)}, u32[]{:S(2)}) copy-start(bf16[8,24,4608]{2,1,0:T(8,128)(2,1)} %get-tuple-element.39) | copy-start | bytes 5308420
  75.3 1.3 copy-start.1
  77.5 1.9 %copy-start.19 = (bf16[8,24,4608]{2,1,0:T(8,128)(2,1)S(1)}, bf16[8,24,4608]{2,1,0:T(8,128)(2,1)}, u32[]{:S(2)}) copy-start(bf16[8,24,4608]{2,1,0:T(8,128)(2,1)} %get-tuple-element.34) | copy-start | bytes 5308420
  140.6 4.2 %copy-start.29 = (bf16[24,4608]{1,0:T(8,128)(2,1)S(1)}, bf16[24,4608]{1,0:T(8,128)(2,1)}, u32[]{:S(2)}) copy-start(bf16[24,4608]{1,0:T(8,128)(2,1)} %copy-done.28) | copy-start | bytes 663556
  140.6 4.2 %copy-start.5 = (f32[24,4608]{1,0:T(8,128)S(1)}, f32[24,4608]{1,0:T(8,128)}, u32[]{:S(2)}) copy-start(f32[24,4608]{1,0:T(8,128)} %copy-done.4) | copy-start | bytes 1327108
  140.6 4.4 %copy-start.22 = (bf16[24,4608]{1,0:T(8,128)(2,1)S(1)}, bf16[24,4608]{1,0:T(8,128)(2,1)}, u32[]{:S(2)}) copy-start(bf16[24,4608]{1,0:T(8,128)(2,1)} %copy-done.21) | copy-start | bytes 663556
  140.6 4.5 %copy-start.35 = (f32[4608]{0:T(1024)S(1)}, f32[4608]{0:T(1024)}, u32[]{:S(2)}) copy-start(f32[4608]{0:T(1024)} %param.12) | copy-start | bytes 55300
  140.7 4.9 %copy-start.24 = (bf16[1,128,4608]{2,1,0:T(8,128)(2,1)S(1)}, bf16[1,128,4608]{2,1,0:T(8,128)(2,1)}, u32[]{:S(2)}) copy-start(bf16[1,128,4608]{2,1,0:T(8,128)(2,1)} %copy-done.23) | copy-start | bytes 3538948
  140.7 4.9 %copy-start.37 = (f32[4608]{0:T(1024)S(1)}, f32[4608]{0:T(1024)}, u32[]{:S(2)}) copy-start(f32[4608]{0:T(1024)} %param.13) | copy-start | bytes 55300
  145.5 18.3 %copy-start.13 = (f32[1152,128]{1,0:T(8,128)S(1)}, f32[1152,128]{1,0:T(8,128)}, u32[]{:S(2)}) copy-start(f32[1152,128]{1,0:T(8,128)} %copy-done.12) | copy-start | bytes 1769476
  147.5 17.9 %copy-start.25 = (bf16[128,4608]{1,0:T(8,128)(2,1)}, bf16[128,4608]{1,0:T(8,128)(2,1)S(1)}, u32[]{:S(2)}) copy-start(bf16[128,4608]{1,0:T(8,128)(2,1)S(1)} %scatter_custom_fusion.1) | copy-start | bytes 3538948
  147.5 17.1 %copy-start.11 = (f32[1152,128]{1,0:T(8,128)S(1)}, f32[1152,128]{1,0:T(8,128)}, u32[]{:S(2)}) copy-start(f32[1152,128]{1,0:T(8,128)} %copy-done.10) | copy-start | bytes 1769476
  163.8 1.6 copy-start.9
  164.6 1.6 copy-start.7
  (17 other events, 15.1 us)

commit v3 on v2

--- a/solution.py
+++ b/solution.py
@@ -302,6 +302,65 @@
         ),
         name="total",
     )(x)
+
+
+def middle_kernel(
+    n_fsdp, rows, d_mix, allowed, w_query, w_key, w_value, w_out, mixed, normed, stack, out_grad,
+    out_full
+):
+    head, width = out_full.shape
+    share = width // n_fsdp
+    low = jnp.bfloat16
+    for f in range(n_fsdp):
+        out_full[:, f * share : (f + 1) * share] = w_out[f]
+    queries = jnp.dot(rows[...], w_query[...], preferred_element_type=jnp.float32).astype(low)
+    keys = jnp.dot(rows[...], w_key[...], preferred_element_type=jnp.float32).astype(low)
+    vals = jnp.dot(rows[...], w_value[...], preferred_element_type=jnp.float32).astype(low)
+    slope = jnp.tanh(contract_cols(queries, keys) * (QUERY_SCALE / SOFTCAP))
+    powers = jnp.where(allowed[...] > 0.5, jnp.exp(SOFTCAP * slope), 0.0)
+    soft = powers / jnp.sum(powers, axis=1, keepdims=True)
+    weights = soft.astype(low)
+    attended = jnp.dot(weights, vals, preferred_element_type=jnp.float32).astype(low)
+    d_attended = contract_cols(d_mix[...], out_full[...]).astype(low)
+    d_values = contract_rows(weights, d_attended).astype(low)
+    d_probs = contract_cols(d_attended, vals)
+    d_soft = soft * (d_probs - jnp.sum(soft * d_probs, axis=1, keepdims=True))
+    d_raw = (d_soft * (1.0 - slope * slope) * QUERY_SCALE).astype(low)
+    d_queries = jnp.dot(d_raw, keys, preferred_element_type=jnp.float32).astype(low)
+    d_keys = contract_rows(d_raw, queries).astype(low)
+    d_stack = jnp.concatenate([d_queries, d_keys, d_values], axis=1)
+    step = width // 6
+    for c in range(6):
+        part = slice(c * step, (c + 1) * step)
+        mixed[:, part] = jnp.dot(
+            attended, out_full[:, part], preferred_element_type=jnp.float32
+        ).astype(low)
+        in_cols = jnp.concatenate([w_query[part], w_key[part], w_value[part]], axis=1)
+        normed[:, part] = contract_cols(d_stack, in_cols).astype(low)
+        stack[part] = contract_rows(rows[:, part], d_stack).astype(low)
+    grad = contract_rows(attended, d_mix[...]).astype(low)
+    for f in range(n_fsdp):
+        out_grad[f] = grad[:, f * share : (f + 1) * share]
+
+
+def middle(n_fsdp, rows, d_mix, allowed, w_query, w_key, w_value, w_out):
+    slots, width = rows.shape
+    head = w_query.shape[1]
+    low = jnp.bfloat16
+    return pl.pallas_call(
+        functools.partial(middle_kernel, n_fsdp),
+        out_shape=[
+            jax.ShapeDtypeStruct((slots, width), low),
+            jax.ShapeDtypeStruct((slots, width), low),
+            jax.ShapeDtypeStruct((width, 3 * head), low),
+            jax.ShapeDtypeStruct((n_fsdp, head, width // n_fsdp), low),
+        ],
+        in_specs=[pl.BlockSpec(memory_space=pltpu.VMEM)] * 7,
+        out_specs=[pl.BlockSpec(memory_space=pltpu.VMEM)] * 4,
+        scratch_shapes=[pltpu.VMEM((head, width), low)],
+        compiler_params=pltpu.CompilerParams(vmem_limit_bytes=VMEM_LIMIT),
+        name="middle",
+    )(rows, d_mix, allowed, w_query, w_key, w_value, w_out)
 
 
 def body(
@@ -343,54 +402,24 @@
     query_cols = query_g.reshape(width, head_width)
     key_cols = key_g.reshape(width, head_width)
     value_cols = value_g.reshape(width, head_width)
-    out_full = jnp.swapaxes(out_g, 0, 1).reshape(head_width, width)
-    queries = jnp.dot(all_rows, query_cols, preferred_element_type=jnp.float32).astype(jnp.bfloat16)
-    keys_all = jnp.dot(all_rows, key_cols, preferred_element_type=jnp.float32).astype(jnp.bfloat16)
-    values_all = jnp.dot(all_rows, value_cols, preferred_element_type=jnp.float32).astype(
-        jnp.bfloat16
-    )
-    raw_scores = contract_cols(queries, keys_all) * QUERY_SCALE
-    capped = SOFTCAP * jnp.tanh(raw_scores / SOFTCAP)
     order = jnp.arange(slots, dtype=jnp.int32)
     allowed = live[None, :] & ((order[None, :] <= order[:, None]) | ~live[:, None])
-    powers = jnp.where(allowed, jnp.exp(capped), 0.0)
-    softmax_values = powers / jnp.sum(powers, axis=1, keepdims=True)
-    rounded_weights = softmax_values.astype(jnp.bfloat16)
-    attended = jnp.dot(rounded_weights, values_all, preferred_element_type=jnp.float32).astype(
-        jnp.bfloat16
-    )
-    mixed_part = (
-        jnp.dot(attended, out_full, preferred_element_type=jnp.float32)
-        .astype(jnp.bfloat16)
-        .reshape(n_seq, cap, width)
-    )
-    out_part = contract_rows(attended, d_mix_all).astype(jnp.bfloat16)
-    out_part = jnp.swapaxes(out_part.reshape(head_width, n_fsdp, width // n_fsdp), 0, 1)
-    d_attended = contract_cols(d_mix_all, out_full).astype(jnp.bfloat16)
-    d_values = contract_rows(rounded_weights, d_attended).astype(jnp.bfloat16)
-    d_probs = contract_cols(d_attended, values_all)
-    d_soft = softmax_values * (d_probs - jnp.sum(softmax_values * d_probs, axis=1, keepdims=True))
-    d_raw = (d_soft * (1.0 - capped / SOFTCAP * (capped / SOFTCAP)) * QUERY_SCALE).astype(
-        jnp.bfloat16
-    )
-    d_queries = jnp.dot(d_raw, keys_all, preferred_element_type=jnp.float32).astype(jnp.bfloat16)
-    d_keys = contract_rows(d_raw, queries).astype(jnp.bfloat16)
-    d_stack = jnp.concatenate([d_queries, d_keys, d_values], axis=1)
-    stack_part = (
-        contract_rows(all_rows, d_stack)
-        .astype(jnp.bfloat16)
-        .reshape(n_fsdp, width // n_fsdp, 3 * head_width)
-    )
-    total_in = contract_cols(d_queries, query_cols)
-    total_in = total_in + contract_cols(d_keys, key_cols)
-    normed_part = (
-        (total_in + contract_cols(d_values, value_cols))
-        .astype(jnp.bfloat16)
-        .reshape(n_seq, cap, width)
-    )
-    mixed_sum, d_normed, grad_query, grad_key, grad_value, out_grad = reduce(
+    mixed_part, normed_part, stack_part, out_part = middle(
+        n_fsdp,
+        all_rows,
+        d_mix_all,
+        allowed.astype(jnp.float32),
+        query_cols,
+        key_cols,
+        value_cols,
+        out_g,
+    )
+    mixed_part = mixed_part.reshape(n_seq, cap, width)
+    normed_part = normed_part.reshape(n_seq, cap, width)
+    stack_part = stack_part.reshape(n_fsdp, width // n_fsdp, 3 * head_width)
+    mixed_sum, d_normed, grads, out_grad = reduce(
         (seq, seq, fsdp, fsdp),
-        (1, 1, 3, 1),
+        (1, 1, 1, 1),
         (mixed_part, normed_part, stack_part, out_part),
         2,
     )
@@ -405,6 +434,9 @@
         n_seq, n_fsdp, jnp.concatenate([gain_term, router_term]).reshape(2 * width // 128, 128), 3
     ).reshape(2 * width)
     grad_gain, grad_router = sums[:width], sums[width:]
+    grad_query = grads[:, :head_width]
+    grad_key = grads[:, head_width : 2 * head_width]
+    grad_value = grads[:, 2 * head_width :]
     scaled = d_normed * norm_gain
     d_kept = inv_root[:, None] * (scaled - unit * jnp.mean(scaled * unit, axis=1, keepdims=True))
     grad_new = (cot_rows + d_kept + d_logit[:, None] * router_weight).astype(jnp.bfloat16)

time: 168 us -> 154 us (0.917)
  matrix products: 17.6 us -> 0.36 us
  Pallas kernels: 119 us -> 130 us
  local copies, waits for them, and re-layouts: 20.5 us -> 14.1 us
    dot_general x16 -> x0, matrix products: 17.3 us -> none  [the longest x6 4.21 us: contract_cols(): lax.dot_general(left, right, (((1,), (1,)), ((), ())), preferred_element_...]
    pallas_call x0 -> x1, Pallas kernels: none -> 10.7 us  [middle(): pl.pallas_call(functools.partial(middle_kernel, n_fsdp), out_shape=[jax.S...]
    unnamed x89 -> x46, local copies, waits for them, and re-layouts: 13.4 us -> 10.2 us
where the time goes in v3:
time: 154 us
  Pallas kernels  130 us (84%)
  local copies, waits for them, and re-layouts  14.1 us (9%)
  other arithmetic  8.68 us (6%)
    pallas_call x1, Pallas kernels, gather(): pl.pallas_call(functools.partial(gather_kernel, plan, order), out_shape=[...  53.2 us
    pallas_call x1, Pallas kernels, reduce(): pl.pallas_call(functools.partial(reduce_kernel, plan, splits), out_shape=...  50.4 us
    pallas_call x1, Pallas kernels, total(): pl.pallas_call(functools.partial(total_kernel, n_seq, n_fsdp), out_shape=...  15.7 us
    pallas_call x1, Pallas kernels, middle(): pl.pallas_call(functools.partial(middle_kernel, n_fsdp), out_shape=[jax.S...  10.7 us
    unnamed x46, local copies, waits for them, and re-layouts  10.2 us
    scatter x1, other arithmetic, body(): mixed_rows = tokens[0].at[target].set(new_rows, mode='drop')[None]  3.59 us

profile of v3, /device:TPU:0, one launch (start us, length us, event | category | flops | bytes accessed | tf_op | source)
XLA Modules:
  0.0 153.9 jit_solution(10968708066962436202)
XLA Ops:
  0.6 1.4 copy.23
  2.3 0.6 copy-done.20
  2.9 0.6 fusion.34
  3.5 0.7 gather_fusion
  4.9 0.7 gather_fusion.1
  5.8 0.5 copy-done.12
  6.3 1.0 copy-done.2
  7.3 1.0 copy-done.3
  8.2 1.0 copy-done.4
  9.2 1.0 copy-done.5
  10.2 53.2 %gather.13 = (bf16[8,24,4608]{2,1,0:T(8,128)(2,1)}, f32[8,8,128]{2,1,0:T(8,128)S(1)}, bf16[4,1152,128]{2,1,0:T(8,128)(2,1)S(1)}, bf16[4,1152,128]{2,1,0:T(8,128)...) custom-call(bf16[24,4608]{1,0:T(8,128)(2,1)S(1)} %get-tuple-element.59.ref, ...), custom_call_target="tpu_custom_call" | custom-call | tf_op jit(solution)/shard_map/gather/pallas_call | solution.py:124
  63.3 0.6 gt.19
  64.0 0.7 not.8
  64.6 0.7 fusion.32.allowed
  65.4 1.3 copy-done.1
  66.6 10.7 %middle.1 = (bf16[192,4608]{1,0:T(8,128)(2,1)}, bf16[192,4608]{1,0:T(8,128)(2,1)}, bf16[4608,384]{1,0:T(8,128)(2,1)}, bf16[4,128,1152]{2,1,0:T(8,128)(2,1)S(1)}) custom-call(bf16[192,4608]{1,0:T(8,128)(2,1)} %bitcast.51, bf16[192,4608]{1,0:T(8,128)(2,1)} %bitcast.52, f32[192,192]{1,0:T(8,128)S(1)} %fusion.32.allowed, bf16[4608,128]{1,0:T(8,128)(2,1)S(1)} %bitcast.41, ...), custom_call_target="tpu_custom_call" | custom-call | tf_op jit(solution)/shard_map/middle/pallas_call | solution.py:350
  77.3 1.5 copy-done
  78.8 50.4 %reduce.5 = (f32[24,4608]{1,0:T(8,128)S(1)}, f32[24,4608]{1,0:T(8,128)S(1)}, f32[1152,384]{1,0:T(8,128)S(1)}, f32[128,1152]{1,0:T(8,128)S(1)}) custom-call(bf16[8,24,4608]{2,1,0:T(8,128)(2,1)S(1)} %bitcast.40, bf16[8,24,4608]{2,1,0:T(8,128)(2,1)} %bitcast.53, bf16[4,1152,384]{2,1,0:T(8,128)(2,1)} %bitcast.50, bf16[4,128,1152]{2,1,0:T(8,128)(2,1)S(1)} %get-tuple-element.45.refs_3_), custom_call_target="tpu_custom_call" | custom-call | tf_op jit(solution)/shard_map/reduce/pallas_call | solution.py:248
  129.2 3.6 %scatter_custom_fusion = bf16[128,4608]{1,0:T(8,128)(2,1)} fusion(bf16[128,4608]{1,0:T(8,128)(2,1)} %bitcast.48, s32[24]{0:T(128)} %get-tuple-element.61, f32[24,4608]{1,0:T(8,128)S(1)} %get-tuple-element.46, f32[24]{0:T(128)S(1)} %fusion.3, bf16[24,4608]{1,0:T(8,128)(2,1)S(1)} %copy-done.7, pred[24]{0:T(512)(128)(4,1)S(1)} %compare_bitcast_fusion), kind=kCustom, calls=%fused_computation.32 | custom fusion | flops 552960 | bytes 1843320 | tf_op jit(solution)/shard_map/scatter | solution.py:428
  132.8 1.2 fusion.35
  134.7 15.7 %total.1 = f32[72,128]{1,0:T(8,128)S(1)} custom-call(f32[72,128]{1,0:T(8,128)S(1)} %pad_maximum_fusion.x_ref), custom_call_target="tpu_custom_call" | custom-call | tf_op jit(solution)/shard_map/total/pallas_call | solution.py:288
  150.4 1.9 %scatter_custom_fusion.1 = bf16[128,4608]{1,0:T(8,128)(2,1)S(1)} fusion(bf16[128,4608]{1,0:T(8,128)(2,1)S(1)} %bitcast.45, s32[24]{0:T(128)} %get-tuple-element.61, f32[24,4608]{1,0:T(8,128)S(1)} %get-tuple-element.47, f32[4608]{0:T(1024)S(1)} %copy-done.19, f32[24]{0:T(128)S(1)} %subtract_multiply_fusion, f32[24]{0:T(128)S(1)} %broadcast_multiply_fusion, ...), kind=kCustom, calls=%fused_computation.33 | custom fusion | flops 1437696 | bytes 2107392 | tf_op jit(solution)/shard_map/scatter | solution.py:443
  152.4 0.7 slice_bitcast_fusion
  153.1 0.8 copy.24
  (50 shorter events, 2.0 us)
Async XLA Ops:
  0.6 1.6 %copy-start.15 = (bf16[1,128,4608]{2,1,0:T(8,128)(2,1)S(1)}, bf16[1,128,4608]{2,1,0:T(8,128)(2,1)}, u32[]{:S(2)}) copy-start(bf16[1,128,4608]{2,1,0:T(8,128)(2,1)} %param.11) | copy-start | bytes 3538948
  2.3 2.6 %copy-start.8 = (bf16[1,128,4608]{2,1,0:T(8,128)(2,1)}, bf16[1,128,4608]{2,1,0:T(8,128)(2,1)S(1)}, u32[]{:S(2)}) copy-start(bf16[1,128,4608]{2,1,0:T(8,128)(2,1)S(1)} %copy.23) | copy-start | bytes 3538948
  2.3 0.7 copy-start.20
  2.3 1.3 copy-start.18
  2.9 2.9 %copy-start.11 = (bf16[1,128,4608]{2,1,0:T(8,128)(2,1)}, bf16[1,128,4608]{2,1,0:T(8,128)(2,1)S(1)}, u32[]{:S(2)}) copy-start(bf16[1,128,4608]{2,1,0:T(8,128)(2,1)S(1)} %copy.22) | copy-start | bytes 3538948
  4.2 1.4 copy-start.6
  4.6 1.0 copy-start.16
  5.6 0.7 copy-start.12
  6.3 1.0 copy-start.2
  7.3 1.0 copy-start.3
  8.2 1.0 copy-start.4
  9.2 1.0 copy-start.5
  65.4 1.3 copy-start.1
  77.3 1.5 copy-start
  78.8 50.4 %copy-start.7 = (bf16[24,4608]{1,0:T(8,128)(2,1)S(1)}, bf16[24,4608]{1,0:T(8,128)(2,1)}, u32[]{:S(2)}) copy-start(bf16[24,4608]{1,0:T(8,128)(2,1)} %copy-done.6) | copy-start | bytes 663556
  132.8 1.3 copy-start.13
  132.8 1.5 copy-start.17
  134.0 16.4 %copy-start.9 = (bf16[1,128,4608]{2,1,0:T(8,128)(2,1)S(1)}, bf16[1,128,4608]{2,1,0:T(8,128)(2,1)}, u32[]{:S(2)}) copy-start(bf16[1,128,4608]{2,1,0:T(8,128)(2,1)} %copy-done.8) | copy-start | bytes 3538948
  134.0 16.4 %copy-start.14 = (bf16[24,4608]{1,0:T(8,128)(2,1)S(1)}, bf16[24,4608]{1,0:T(8,128)(2,1)}, u32[]{:S(2)}) copy-start(bf16[24,4608]{1,0:T(8,128)(2,1)} %copy-done.12) | copy-start | bytes 663556
  134.0 16.4 %copy-start.19 = (f32[4608]{0:T(1024)S(1)}, f32[4608]{0:T(1024)}, u32[]{:S(2)}) copy-start(f32[4608]{0:T(1024)} %param.13) | copy-start | bytes 55300
  152.4 1.5 copy-start.10

commit v4 on v3

--- a/solution.py
+++ b/solution.py
@@ -63,59 +63,152 @@
     return ref.at[index, :, pl.ds(c * step, step)]
 
 
-def gather_start(axis, size, src, dst, sems, chunks, c):
-    me, outer, inner, outers = place(axis, size)
-    step = src.shape[1] // chunks
-    block = src if chunks == 1 else src.at[:, pl.ds(c * step, step)]
-    land = piece(dst, me, chunks, c)
-    first = []
-    for d in range(1, outers):
-        peer = {axis: lax.rem(outer + d, outers) * 2 + inner}
-        first.append(remote(block, land, sems.at[0, d, c], sems.at[1, d, c], peer))
-    partner = {axis: outer * 2 + 1 - inner}
-    second = [remote(block, land, sems.at[2, 0, c], sems.at[3, 0, c], partner)]
-    for copy in first + second:
-        copy.start()
-    return first, second
-
-
-def gather_forward(axis, size, dst, sems, copies, chunks, c):
-    me, outer, inner, outers = place(axis, size)
-    first, second = copies
-    partner = {axis: outer * 2 + 1 - inner}
-    for d in range(1, outers):
-        first[d - 1].wait_recv()
-        land = piece(dst, lax.rem(outer + outers - d, outers) * 2 + inner, chunks, c)
-        copy = remote(land, land, sems.at[2, d, c], sems.at[3, d, c], partner)
-        copy.start()
-        second.append(copy)
+class Line:
+    def __init__(self, axis, size, src, dst, sems, chunks, c, early):
+        self.axis, self.dst, self.sems, self.chunks, self.c = axis, dst, sems, chunks, c
+        self.me, self.outer, self.inner, self.outers = place(axis, size)
+        step = src.shape[1] // chunks
+        self.src = src if chunks == 1 else src.at[:, pl.ds(c * step, step)]
+        self.kinds = (0, 1) if early else (0,)
+        self.early = early
+        self.partner = {axis: self.outer * 2 + 1 - self.inner}
+
+    def land(self, kind, side, k):
+        at = self.outer - k if side == 0 else self.outer + k
+        parity = self.inner if kind == 0 else 1 - self.inner
+        return piece(self.dst, at * 2 + parity, self.chunks, self.c)
+
+    def have(self, side, k):
+        return self.outer >= k if side == 0 else self.outer + k < self.outers
+
+    def goes(self, side):
+        return self.outer < self.outers - 1 if side == 0 else self.outer > 0
+
+    def hop(self, kind, side, k):
+        land = self.land(kind, side, k)
+        to = self.outer + 1 if side == 0 else self.outer - 1
+        return remote(
+            self.src if kind == 0 and k == 0 else land,
+            land,
+            self.sems.at[kind, 2 * side, k, self.c],
+            self.sems.at[kind, 2 * side + 1, k + 1, self.c],
+            {self.axis: to * 2 + self.inner},
+        )
+
+    def arrival(self, kind, side, k):
+        land = self.land(kind, side, k)
+        return remote(
+            land,
+            land,
+            self.sems.at[kind, 2 * side, k, self.c],
+            self.sems.at[kind, 2 * side + 1, k, self.c],
+            self.partner,
+        )
+
+    def across(self, side, k):
+        land = self.land(0, side, k)
+        return remote(
+            self.src if k == 0 else land,
+            land,
+            self.sems.at[2, 2 * side, k, self.c],
+            self.sems.at[2, 2 * side + 1, k, self.c],
+            self.partner,
+        )
+
+    def across_arrival(self, side, k):
+        land = self.land(1, side, k)
+        return remote(
+            land,
+            land,
+            self.sems.at[2, 2 * side, k, self.c],
+            self.sems.at[2, 2 * side + 1, k, self.c],
+            self.partner,
+        )
+
+    def start(self):
+        self.across(0, 0).start()
+        for side in (0, 1):
+            pl.when(self.goes(side))(self.hop(0, side, 0).start)
+
+    def step(self, k):
+        if k == 0:
+            if self.early:
+                self.across_arrival(0, 0).wait_recv()
+                for side in (0, 1):
+                    pl.when(self.goes(side))(self.hop(1, side, 0).start)
+            return
+        for side in (0, 1):
+            for kind in self.kinds:
+
+                @pl.when(self.have(side, k))
+                def _(side=side, kind=kind):
+                    self.arrival(kind, side, k).wait_recv()
+                    if k < self.outers - 1:
+                        pl.when(self.goes(side))(self.hop(kind, side, k).start)
+                    if not self.early:
+                        self.across(side, k).start()
+
+    def finish(self):
+        self.across(0, 0).wait_send()
+        if not self.early:
+            self.across_arrival(0, 0).wait_recv()
+        for side in (0, 1):
+            for k in range(self.outers - 1):
+                for kind in self.kinds:
+                    pl.when(jnp.logical_and(self.have(side, k), self.goes(side)))(
+                        self.hop(kind, side, k).wait_send
+                    )
+            if not self.early:
+                for k in range(1, self.outers):
+
+                    @pl.when(self.have(side, k))
+                    def _(side=side, k=k):
+                        self.across(side, k).wait_send()
+                        self.across_arrival(side, k).wait_recv()
+
+
+def meet_lines(sizes):
+    barrier = pltpu.get_barrier_semaphore()
+    count = 0
+    for axis, size in sizes.items():
+        me, outer, inner, outers = place(axis, size)
+        pl.semaphore_signal(
+            barrier, inc=1, device_id={axis: outer * 2 + 1 - inner}, device_id_type=MESH
+        )
+        for there, to in ((outer < outers - 1, outer + 1), (outer > 0, outer - 1)):
+
+            @pl.when(there)
+            def _(axis=axis, inner=inner, to=to):
+                pl.semaphore_signal(
+                    barrier, inc=1, device_id={axis: to * 2 + inner}, device_id_type=MESH
+                )
+
+            count = count + there.astype(jnp.int32)
+        count = count + 1
+    pl.semaphore_wait(barrier, count)
 
 
 def gather_kernel(plan, order, *refs):
     count = len(plan)
     srcs, dsts = refs[:count], refs[count : 2 * count]
     sems, own_sems = refs[2 * count : 3 * count], refs[3 * count]
-    peers = []
-    for axis, size in dict(p[:2] for p in plan).items():
-        peers += pair_peers(axis, size)
-    meet(peers)
-    running = []
+    meet_lines(dict(p[:2] for p in plan))
+    lines = []
     for i, c in order:
-        axis, size, chunks = plan[i]
-        running.append(gather_start(axis, size, srcs[i], dsts[i], sems[i], chunks, c))
+        axis, size, chunks, early = plan[i]
+        lines.append(Line(axis, size, srcs[i], dsts[i], sems[i], chunks, c, c < early))
+    for line in lines:
+        line.start()
     owns = []
-    for i, (axis, size, _) in enumerate(plan):
-        own = pltpu.make_async_copy(srcs[i], dsts[i].at[lax.axis_index(axis)], own_sems.at[i])
+    for i, p in enumerate(plan):
+        own = pltpu.make_async_copy(srcs[i], dsts[i].at[lax.axis_index(p[0])], own_sems.at[i])
         own.start()
         owns.append(own)
-    for (i, c), copies in zip(order, running):
-        axis, size, chunks = plan[i]
-        gather_forward(axis, size, dsts[i], sems[i], copies, chunks, c)
-    for first, second in running:
-        for copy in first:
-            copy.wait_send()
-        for copy in second:
-            copy.wait()
+    steps = [(j + k, j, k) for j, line in enumerate(lines) for k in range(line.outers)]
+    for _, j, k in sorted(steps):
+        lines[j].step(k)
+    for line in lines:
+        line.finish()
     for own in owns:
         own.wait()
 
@@ -128,7 +221,9 @@
         ],
         in_specs=[pl.BlockSpec(memory_space=pl.ANY)] * len(arrays),
         out_specs=[pl.BlockSpec(memory_space=pl.ANY)] * len(arrays),
-        scratch_shapes=[pltpu.SemaphoreType.DMA((4, size // 2, chunks)) for _, size, chunks in plan]
+        scratch_shapes=[
+            pltpu.SemaphoreType.DMA((3, 4, p[1] // 2, p[2])) for p in plan
+        ]
         + [pltpu.SemaphoreType.DMA((len(arrays),))],
         compiler_params=pltpu.CompilerParams(
             collective_id=collective_id, has_side_effects=True, vmem_limit_bytes=VMEM_LIMIT
@@ -389,9 +484,17 @@
     d_mix = (gate_value[:, None] * cot_rows).astype(jnp.bfloat16)
     seq, fsdp = ("seq", n_seq), ("fsdp", n_fsdp)
     rows_g, flags_g, query_g, key_g, value_g, out_g, d_mix_g = gather(
-        (seq + (3,), seq + (1,), fsdp + (1,), fsdp + (1,), fsdp + (1,), fsdp + (1,), seq + (3,)),
         (
-            (1, 0), (0, 0), (2, 0), (0, 1), (3, 0), (0, 2), (4, 0), (6, 0), (5, 0), (6, 1), (6, 2)
+            seq + (3, 1),
+            seq + (1, 0),
+            fsdp + (1, 0),
+            fsdp + (1, 0),
+            fsdp + (1, 0),
+            fsdp + (1, 0),
+            seq + (3, 1),
+        ),
+        (
+            (0, 0), (1, 0), (2, 0), (0, 1), (3, 0), (0, 2), (4, 0), (6, 0), (5, 0), (6, 1), (6, 2)
         ),
         (sending, flags, w_query, w_key, w_value, w_out, d_mix),
         1,

time: 154 us -> 156 us (1.013)
  Pallas kernels: 130 us -> 132 us
    pallas_call x1, Pallas kernels: 50.4 us -> 45.6 us  [reduce(): pl.pallas_call(functools.partial(reduce_kernel, plan, splits), out_shape=...]
    pallas_call x1, Pallas kernels: 53.2 us -> 57.5 us  [gather(): pl.pallas_call(functools.partial(gather_kernel, plan, order), out_shape=[...]
    pallas_call x1, Pallas kernels: 15.7 us -> 18 us  [total(): pl.pallas_call(functools.partial(total_kernel, n_seq, n_fsdp), out_shape=...]
where the time goes in v4:
time: 156 us
  Pallas kernels  132 us (85%)
  local copies, waits for them, and re-layouts  14.1 us (9%)
  other arithmetic  8.68 us (6%)
    pallas_call x1, Pallas kernels, gather(): pl.pallas_call(functools.partial(gather_kernel, plan, order), out_shape=[...  57.5 us
    pallas_call x1, Pallas kernels, reduce(): pl.pallas_call(functools.partial(reduce_kernel, plan, splits), out_shape=...  45.6 us
    pallas_call x1, Pallas kernels, total(): pl.pallas_call(functools.partial(total_kernel, n_seq, n_fsdp), out_shape=...  18 us
    pallas_call x1, Pallas kernels, middle(): pl.pallas_call(functools.partial(middle_kernel, n_fsdp), out_shape=[jax.S...  10.7 us
    unnamed x46, local copies, waits for them, and re-layouts  10.2 us
    scatter x1, other arithmetic, body(): mixed_rows = tokens[0].at[target].set(new_rows, mode='drop')[None]  3.59 us

profile of v4, /device:TPU:0, one launch (start us, length us, event | category | flops | bytes accessed | tf_op | source)
XLA Modules:
  0.0 155.8 jit_solution(602795620973796368)
XLA Ops:
  0.6 1.4 copy.23
  2.3 0.6 copy-done.20
  2.9 0.6 fusion.34
  3.5 0.7 gather_fusion
  4.9 0.7 gather_fusion.1
  5.8 0.5 copy-done.12
  6.3 1.0 copy-done.2
  7.3 1.0 copy-done.3
  8.2 1.0 copy-done.4
  9.2 1.0 copy-done.5
  10.2 57.5 %gather.13 = (bf16[8,24,4608]{2,1,0:T(8,128)(2,1)}, f32[8,8,128]{2,1,0:T(8,128)S(1)}, bf16[4,1152,128]{2,1,0:T(8,128)(2,1)S(1)}, bf16[4,1152,128]{2,1,0:T(8,128)...) custom-call(bf16[24,4608]{1,0:T(8,128)(2,1)S(1)} %get-tuple-element.59.ref, ...), custom_call_target="tpu_custom_call" | custom-call | tf_op jit(solution)/shard_map/gather/pallas_call | solution.py:217
  67.7 0.6 gt.19
  68.3 0.7 not.8
  68.9 0.7 fusion.32.allowed
  69.7 1.3 copy-done.1
  71.0 10.7 %middle.1 = (bf16[192,4608]{1,0:T(8,128)(2,1)}, bf16[192,4608]{1,0:T(8,128)(2,1)}, bf16[4608,384]{1,0:T(8,128)(2,1)}, bf16[4,128,1152]{2,1,0:T(8,128)(2,1)S(1)}) custom-call(bf16[192,4608]{1,0:T(8,128)(2,1)} %bitcast.51, bf16[192,4608]{1,0:T(8,128)(2,1)} %bitcast.52, f32[192,192]{1,0:T(8,128)S(1)} %fusion.32.allowed, bf16[4608,128]{1,0:T(8,128)(2,1)S(1)} %bitcast.41, ...), custom_call_target="tpu_custom_call" | custom-call | tf_op jit(solution)/shard_map/middle/pallas_call | solution.py:445
  81.6 1.5 copy-done
  83.1 45.6 %reduce.5 = (f32[24,4608]{1,0:T(8,128)S(1)}, f32[24,4608]{1,0:T(8,128)S(1)}, f32[1152,384]{1,0:T(8,128)S(1)}, f32[128,1152]{1,0:T(8,128)S(1)}) custom-call(bf16[8,24,4608]{2,1,0:T(8,128)(2,1)S(1)} %bitcast.40, bf16[8,24,4608]{2,1,0:T(8,128)(2,1)} %bitcast.53, bf16[4,1152,384]{2,1,0:T(8,128)(2,1)} %bitcast.50, bf16[4,128,1152]{2,1,0:T(8,128)(2,1)S(1)} %get-tuple-element.45.refs_3_), custom_call_target="tpu_custom_call" | custom-call | tf_op jit(solution)/shard_map/reduce/pallas_call | solution.py:343
  128.8 3.6 %scatter_custom_fusion = bf16[128,4608]{1,0:T(8,128)(2,1)} fusion(bf16[128,4608]{1,0:T(8,128)(2,1)} %bitcast.48, s32[24]{0:T(128)} %get-tuple-element.61, f32[24,4608]{1,0:T(8,128)S(1)} %get-tuple-element.46, f32[24]{0:T(128)S(1)} %fusion.3, bf16[24,4608]{1,0:T(8,128)(2,1)S(1)} %copy-done.7, pred[24]{0:T(512)(128)(4,1)S(1)} %compare_bitcast_fusion), kind=kCustom, calls=%fused_computation.32 | custom fusion | flops 552960 | bytes 1843320 | tf_op jit(solution)/shard_map/scatter | solution.py:531
  132.4 1.2 fusion.35
  134.3 18.0 %total.1 = f32[72,128]{1,0:T(8,128)S(1)} custom-call(f32[72,128]{1,0:T(8,128)S(1)} %pad_maximum_fusion.x_ref), custom_call_target="tpu_custom_call" | custom-call | tf_op jit(solution)/shard_map/total/pallas_call | solution.py:383
  152.4 1.9 %scatter_custom_fusion.1 = bf16[128,4608]{1,0:T(8,128)(2,1)S(1)} fusion(bf16[128,4608]{1,0:T(8,128)(2,1)S(1)} %bitcast.45, s32[24]{0:T(128)} %get-tuple-element.61, f32[24,4608]{1,0:T(8,128)S(1)} %get-tuple-element.47, f32[4608]{0:T(1024)S(1)} %copy-done.19, f32[24]{0:T(128)S(1)} %subtract_multiply_fusion, f32[24]{0:T(128)S(1)} %broadcast_multiply_fusion, ...), kind=kCustom, calls=%fused_computation.33 | custom fusion | flops 1437696 | bytes 2107392 | tf_op jit(solution)/shard_map/scatter | solution.py:546
  154.3 0.7 slice_bitcast_fusion
  155.0 0.8 copy.24
  (50 shorter events, 2.0 us)
Async XLA Ops:
  0.6 1.6 %copy-start.15 = (bf16[1,128,4608]{2,1,0:T(8,128)(2,1)S(1)}, bf16[1,128,4608]{2,1,0:T(8,128)(2,1)}, u32[]{:S(2)}) copy-start(bf16[1,128,4608]{2,1,0:T(8,128)(2,1)} %param.11) | copy-start | bytes 3538948
  2.3 2.6 %copy-start.8 = (bf16[1,128,4608]{2,1,0:T(8,128)(2,1)}, bf16[1,128,4608]{2,1,0:T(8,128)(2,1)S(1)}, u32[]{:S(2)}) copy-start(bf16[1,128,4608]{2,1,0:T(8,128)(2,1)S(1)} %copy.23) | copy-start | bytes 3538948
  2.3 0.7 copy-start.20
  2.3 1.3 copy-start.18
  2.9 2.9 %copy-start.11 = (bf16[1,128,4608]{2,1,0:T(8,128)(2,1)}, bf16[1,128,4608]{2,1,0:T(8,128)(2,1)S(1)}, u32[]{:S(2)}) copy-start(bf16[1,128,4608]{2,1,0:T(8,128)(2,1)S(1)} %copy.22) | copy-start | bytes 3538948
  4.2 1.4 copy-start.6
  4.6 1.0 copy-start.16
  5.6 0.7 copy-start.12
  6.3 1.0 copy-start.2
  7.3 1.0 copy-start.3
  8.2 1.0 copy-start.4
  9.2 1.0 copy-start.5
  69.7 1.3 copy-start.1
  81.6 1.5 copy-start
  83.1 45.6 %copy-start.7 = (bf16[24,4608]{1,0:T(8,128)(2,1)S(1)}, bf16[24,4608]{1,0:T(8,128)(2,1)}, u32[]{:S(2)}) copy-start(bf16[24,4608]{1,0:T(8,128)(2,1)} %copy-done.6) | copy-start | bytes 663556
  132.4 1.3 copy-start.13
  132.4 1.5 copy-start.17
  133.6 18.8 %copy-start.9 = (bf16[1,128,4608]{2,1,0:T(8,128)(2,1)S(1)}, bf16[1,128,4608]{2,1,0:T(8,128)(2,1)}, u32[]{:S(2)}) copy-start(bf16[1,128,4608]{2,1,0:T(8,128)(2,1)} %copy-done.8) | copy-start | bytes 3538948
  133.6 18.8 %copy-start.14 = (bf16[24,4608]{1,0:T(8,128)(2,1)S(1)}, bf16[24,4608]{1,0:T(8,128)(2,1)}, u32[]{:S(2)}) copy-start(bf16[24,4608]{1,0:T(8,128)(2,1)} %copy-done.12) | copy-start | bytes 663556
  133.6 18.8 %copy-start.19 = (f32[4608]{0:T(1024)S(1)}, f32[4608]{0:T(1024)}, u32[]{:S(2)}) copy-start(f32[4608]{0:T(1024)} %param.13) | copy-start | bytes 55300
  154.3 1.5 copy-start.10
